TPU v7x, 256 devices: a whole 4x4x8 slice. The times are simulated.
256 devices in a mesh: ctx: 64 (over y, z, core), tp: 4 (over x).
Axes of the slice: x: 4, y: 4, z: 8, core: 2. Of those that a mesh axis runs over, the one named last changes fastest.
Arguments:
- qkv: bfloat16 [3, 16384, 4096], P(None, 'ctx', 'tp'), may hold values from -6 to 6
- short_taps: float32 [3, 3, 4096], P(None, None, 'tp'), may hold values from -3 to 3
- long_filter: bfloat16 [16384, 4096], P('ctx', 'tp'), may hold values from -0.046875 to 0.046875
- skip: float32 [4096], P('tp'), may hold values from 0.5 to 1.5
- out_weight: bfloat16 [4096, 4096], P('tp'), may hold values from -0.09375 to 0.09375
Outputs:
- mixed: bfloat16 [16384, 4096], P('ctx', 'tp')
All inputs are finite; a program needn't handle non-finite values.
Results may differ from a plain program's by a relative error of at most 0.024.
Values may be sent and summed in bfloat16 or wider, within the bound.
A program may use at most 128 MiB of HBM per device.

v0:
```python
import math

import jax
import jax.numpy as jnp
from jax import lax
from jax.sharding import PartitionSpec as P


def passed_along(value, axis, steps):
    count = lax.axis_size(axis)
    first, last = (max(0, -steps), min(count, count - steps))
    return lax.ppermute(value, axis, [(source, source + steps) for source in range(first, last)])


def cycle_tables(shards):
    freqs = jnp.arange(2 * shards, dtype=jnp.int32)[:, None]
    anchor = jnp.arange(shards, dtype=jnp.int32)[None, :]
    phase = freqs * anchor % (2 * shards)
    angle = phase.astype(jnp.float32) * (2.0 * math.pi / (2 * shards))
    return (jnp.cos(angle).astype(jnp.bfloat16), (-jnp.sin(angle)).astype(jnp.bfloat16))


def column_tables(device, shards, tok_rows):
    points = 2 * tok_rows * shards
    lead_freq = jnp.arange(2, dtype=jnp.int32)[:, None, None] + 2 * device
    inner_freq = jnp.arange(tok_rows, dtype=jnp.int32)[None, :, None]
    offset = jnp.arange(tok_rows, dtype=jnp.int32)[None, None, :]
    phase = (offset * inner_freq % tok_rows * (2 * shards) + offset * lead_freq) % points
    angle = phase.astype(jnp.float32) * (2.0 * math.pi / points)
    return (jnp.cos(angle).astype(jnp.bfloat16), (-jnp.sin(angle)).astype(jnp.bfloat16))


def complex_product(left_real, left_imag, right_real, right_imag):
    left_real = left_real.astype(jnp.float32)
    left_imag = left_imag.astype(jnp.float32)
    right_real = right_real.astype(jnp.float32)
    right_imag = right_imag.astype(jnp.float32)
    out_real = left_real * right_real - left_imag * right_imag
    out_imag = left_real * right_imag + left_imag * right_real
    return (out_real.astype(jnp.bfloat16), out_imag.astype(jnp.bfloat16))


def body(qkv, short_taps, long_filter, skip, out_weight):
    shards = lax.axis_size("ctx")
    device = lax.axis_index("ctx")
    tok_rows = qkv.shape[1]
    channels = qkv.shape[2]
    piece_rows = tok_rows // shards
    points = 2 * tok_rows * shards
    f32 = jnp.float32
    edge = passed_along(qkv[:, tok_rows - 2 :, :], "ctx", 1)
    padded = jnp.concatenate([edge, qkv], axis=1).astype(f32)
    shortened = (
        short_taps[:, 0][:, None, :] * padded[:, 2:]
        + short_taps[:, 1][:, None, :] * padded[:, 1:-1]
        + short_taps[:, 2][:, None, :] * padded[:, :-2]
    )
    signal = (shortened[1] * shortened[2]).astype(jnp.bfloat16)
    cycle_cos, cycle_sin = cycle_tables(shards)
    col_cos, col_sin = column_tables(device, shards, tok_rows)
    stacked = jnp.stack([signal, long_filter])[:, None]
    spread = lax.all_to_all(stacked, "ctx", split_axis=2, concat_axis=1, tiled=True)
    first_real = jnp.einsum("kr,srjc->skjc", cycle_cos, spread, preferred_element_type=f32)
    first_imag = jnp.einsum("kr,srjc->skjc", cycle_sin, spread, preferred_element_type=f32)
    combined = jnp.stack([first_real, first_imag], axis=1).astype(jnp.bfloat16)
    combined = combined.reshape(4, 2 * shards, piece_rows, channels)
    gathered = lax.all_to_all(combined, "ctx", split_axis=1, concat_axis=2, tiled=True)
    part_real = gathered[0::2]
    part_imag = gathered[1::2]
    spec_real = (
        jnp.einsum("lkj,sljc->slkc", col_cos, part_real, preferred_element_type=f32)
        - jnp.einsum("lkj,sljc->slkc", col_sin, part_imag, preferred_element_type=f32)
    ).astype(jnp.bfloat16)
    spec_imag = (
        jnp.einsum("lkj,sljc->slkc", col_cos, part_imag, preferred_element_type=f32)
        + jnp.einsum("lkj,sljc->slkc", col_sin, part_real, preferred_element_type=f32)
    ).astype(jnp.bfloat16)
    packed = jnp.stack([spec_real, spec_imag], axis=1).reshape(4, 2, tok_rows, channels)
    natural = lax.all_to_all(packed, "ctx", split_axis=2, concat_axis=1, tiled=True)
    prod_real, prod_imag = complex_product(natural[0], natural[1], natural[2], natural[3])
    returned = lax.all_to_all(
        jnp.stack([prod_real, prod_imag]), "ctx", split_axis=1, concat_axis=2, tiled=True
    )
    prod_real = returned[0]
    prod_imag = returned[1]
    back_real = jnp.einsum(
        "lkj,lkc->ljc", col_cos, prod_real, preferred_element_type=f32
    ) + jnp.einsum("lkj,lkc->ljc", col_sin, prod_imag, preferred_element_type=f32)
    back_imag = jnp.einsum(
        "lkj,lkc->ljc", col_cos, prod_imag, preferred_element_type=f32
    ) - jnp.einsum("lkj,lkc->ljc", col_sin, prod_real, preferred_element_type=f32)
    back = jnp.stack([back_real, back_imag]).astype(jnp.bfloat16)
    regrouped = lax.all_to_all(back, "ctx", split_axis=2, concat_axis=1, tiled=True)
    conv_rows = jnp.einsum(
        "kr,kjc->rjc", cycle_cos, regrouped[0], preferred_element_type=f32
    ) + jnp.einsum("kr,kjc->rjc", cycle_sin, regrouped[1], preferred_element_type=f32)
    conv_rows = (conv_rows * (1.0 / points)).astype(jnp.bfloat16)
    homed = lax.all_to_all(conv_rows, "ctx", split_axis=0, concat_axis=1, tiled=True).reshape(
        tok_rows, channels
    )
    gated = (shortened[0] * (homed.astype(f32) + skip * signal.astype(f32))).astype(jnp.bfloat16)
    terms = jnp.dot(gated, out_weight, preferred_element_type=f32)
    return lax.psum_scatter(terms.astype(jnp.bfloat16), "tp", scatter_dimension=1, tiled=True)


def solution(mesh):
    placed = (P(None, "ctx", "tp"), P(None, None, "tp"), P("ctx", "tp"), P("tp"), P("tp", None))
    return jax.shard_map(
        body, mesh=mesh, in_specs=placed, out_specs=P("ctx", "tp"), check_vma=False
    )
```

profile of v0, /device:TPU:1, one launch (start us, length us, event | category | flops | bytes accessed | tf_op | source)
XLA Modules:
  0.0 559.1 jit_solution(1452441870775057515)
XLA Ops:
  6.5 0.8 slice.69
  7.4 4.9 collective-permute-start
  12.3 0.9 fusion.67
  13.3 1.9 maximum_convert_fusion
  15.2 0.9 fusion
  16.1 0.1 fusion.12
  16.3 0.8 copy-done.3
  17.1 0.5 copy-done.4
  17.5 0.1 maximum_bitcast_fusion
  17.6 0.3 copy-done.1
  17.9 1.1 copy.31
  19.0 41.8 %all_to_all.84 = bf16[2,1,256,1024]{3,0,1,2:T(2,128)(2,1)S(1)} all-to-all(bf16[2,1,256,1024]{3,0,1,2:T(2,128)(2,1)S(1)} %copy.31), channel_id=1, replica_groups=mesh['ctx'=64,'tp'=4] {'ctx'}, dimensions={2} | all-to-all | bytes 2097152 | tf_op jit(solution)/shard_map/all_to_all | solution.py:62
  60.8 1.8 convert_bitcast_fusion
  62.6 1.8 convert_bitcast_fusion.1
  64.4 2.3 pad_maximum_fusion
  66.7 6.3 %copy.34 = bf16[2,2,128,4,1024]{4,2,3,1,0:T(8,128)(2,1)} copy(bf16[2,2,128,4,1024]{2,4,3,0,1:T(8,128)(2,1)} %pad_maximum_fusion) | data formatting | bytes 8388608 | tf_op jit(solution)/shard_map/stack | solution.py:65
  73.0 7.4 %copy.35 = bf16[4,128,4,1024]{3,2,0,1:T(4,128)(2,1)} copy(bf16[4,128,4,1024]{3,1,2,0:T(8,128)(2,1)} %bitcast.112) | data formatting | bytes 8388608 | tf_op jit(solution)/shard_map/convert_element_type | solution.py:65
  80.4 6.4 %all-to-all-start.1 = ((bf16[4,128,4,1024]{3,2,0,1:T(4,128)(2,1)}), bf16[4,128,4,1024]{3,2,0,1:T(4,128)(2,1)}, u32[]{:S(2)}, u32[]{:S(2)}) async-start(bf16[4,128,4,1024]{3,2,0,1:T(4,128)(2,1)} %copy.35), calls=%async_computation.1 | async-start | bytes 8388608 | tf_op jit(solution)/shard_map/all_to_all | solution.py:67
  86.8 0.0 reduce-scatter.2.cloned.1.call-start
  86.8 0.1 fusion.25
  87.0 0.1 iota_multiply_fusion
  87.0 95.6 %all-to-all-done.1 = bf16[4,128,4,1024]{3,2,0,1:T(4,128)(2,1)} async-done(((bf16[4,128,4,1024]{3,2,0,1:T(4,128)(2,1)}), bf16[4,128,4,1024]{3,2,0,1:T(4,128)(2,1)}, u32[]{:S(2)}, u32[]{:S(2)}) %all-to-all-start.1) | async-done | bytes 4194336 | tf_op jit(solution)/shard_map/all_to_all | solution.py:67
  182.7 10.6 %copy.37 = bf16[4,2,64,4,1024]{4,1,3,2,0:T(2,128)(2,1)} copy(bf16[4,2,64,4,1024]{4,3,0,1,2:T(4,128)(2,1)} %bitcast.16) | data formatting | bytes 8388608 | tf_op jit(solution)/shard_map/all_to_all | solution.py:67
  193.3 6.3 %fusion.64 = (bf16[2,2,256,1024]{3,1,2,0:T(2,128)(2,1)}, bf16[2,2,256,1024]{3,1,2,0:T(2,128)(2,1)}) fusion(bf16[4,2,256,1024]{3,1,2,0:T(2,128)(2,1)} %bitcast.110), kind=kLoop, calls=%fused_computation.109 | loop fusion | bytes 8388608 | tf_op jit(solution)/shard_map/slice | solution.py:68
  199.6 4.7 copy.72
  204.2 6.1 %copy.73 = bf16[2,2,256,1024]{2,3,0,1:T(8,128)(2,1)} copy(bf16[2,2,256,1024]{3,1,2,0:T(2,128)(2,1)} %get-tuple-element.8) | data formatting | bytes 4194304
  210.4 4.1 fusion.28
  214.5 2.6 fusion.30
  217.1 3.0 fusion.7
  220.1 2.9 fusion.6
  223.0 2.3 pad_maximum_fusion.1
  225.4 6.7 %copy.44 = bf16[2,2,2,256,1024]{4,3,2,1,0:T(8,128)(2,1)} copy(bf16[2,2,2,256,1024]{3,4,0,2,1:T(8,128)(2,1)} %pad_maximum_fusion.1) | data formatting | bytes 8388608 | tf_op jit(solution)/shard_map/stack | solution.py:78
  232.1 8.6 %copy.45 = bf16[4,2,256,1024]{3,1,0,2:T(2,128)(2,1)} copy(bf16[4,2,256,1024]{3,2,1,0:T(8,128)(2,1)} %bitcast.113) | data formatting | bytes 8388608 | tf_op jit(solution)/shard_map/reshape | solution.py:78
  240.6 102.2 %all_to_all.85 = bf16[4,2,256,1024]{3,1,0,2:T(2,128)(2,1)S(1)} all-to-all(bf16[4,2,256,1024]{3,1,0,2:T(2,128)(2,1)} %copy.45), channel_id=1, replica_groups=mesh['ctx'=64,'tp'=4] {'ctx'}, dimensions={2} | all-to-all | bytes 8388608 | tf_op jit(solution)/shard_map/all_to_all | solution.py:79
  342.8 5.4 copy.83
  348.2 2.0 fusion.3
  350.2 1.5 pad_maximum_fusion.2
  351.7 1.3 copy.47
  353.0 57.1 %all_to_all.86 = bf16[2,128,4,1024]{3,2,0,1:T(4,128)(2,1)S(1)} all-to-all(bf16[2,128,4,1024]{3,2,0,1:T(4,128)(2,1)S(1)} %copy.47), channel_id=1, replica_groups=mesh['ctx'=64,'tp'=4] {'ctx'}, dimensions={1} | all-to-all | bytes 4194304 | tf_op jit(solution)/shard_map/all_to_all | solution.py:81
  410.0 0.7 copy.48
  410.8 2.0 fusion.66
  412.8 0.4 copy.49
  413.1 0.3 squeeze.22
  413.4 1.6 copy.50
  415.0 0.3 squeeze.23
  415.3 2.2 fusion.63
  417.5 2.2 fusion.62
  419.8 2.6 fusion.10
  422.4 2.6 fusion.9
  425.1 0.2 pad_maximum_fusion.3
  425.3 2.2 copy.51
  427.4 57.1 %all_to_all.87 = bf16[2,2,256,1024]{3,1,0,2:T(2,128)(2,1)S(1)} all-to-all(bf16[2,2,256,1024]{3,1,0,2:T(2,128)(2,1)S(1)} %copy.51), channel_id=1, replica_groups=mesh['ctx'=64,'tp'=4] {'ctx'}, dimensions={2} | all-to-all | bytes 4194304 | tf_op jit(solution)/shard_map/all_to_all | solution.py:93
  484.5 1.4 copy.84
  485.9 1.5 fusion.65
  487.4 0.4 squeeze.25
  487.9 0.4 squeeze.24
  488.3 0.4 fusion.44
  488.8 0.4 fusion.11
  489.2 0.4 copy.53
  489.6 23.2 %all_to_all.88 = bf16[64,4,1024]{2,1,0:T(4,128)(2,1)} all-to-all(bf16[64,4,1024]{2,1,0:T(4,128)(2,1)S(1)} %copy.53), channel_id=1, replica_groups=mesh['ctx'=64,'tp'=4] {'ctx'}, dimensions={0} | all-to-all | bytes 1048576 | tf_op jit(solution)/shard_map/all_to_all | solution.py:98
  512.8 2.1 reshape.191
  514.9 7.6 %convolution_convert_fusion = bf16[256,4096]{1,0:T(8,128)(2,1)} fusion(bf16[1024,4096]{1,0:T(8,128)(2,1)} %param.9, f32[3,256,1024]{2,1,0:T(8,128)S(1)} %copy-done.2, f32[256,1024]{1,0:T(8,128)} %reshape.191, bf16[1,256,1024]{2,1,0:T(8,128)(2,1)} %copy-done.3, f32[1024]{0:T(1024)S(1)} %copy-done.5), kind=kOutput, calls=%fused_computation | convolution fusion | flops 2149842944 | bytes 13111296 | tf_op jit(solution)/shard_map/dot_general | solution.py:102
  522.5 0.0 reduce-scatter.2.cloned.1.call-update
  522.5 29.3 %reduce-scatter.2.cloned.1.call-done = bf16[256,1024]{1,0:T(8,128)(2,1)} async-done(((bf16[256,4096]{1,0:T(8,128)(2,1)}), bf16[256,1024]{1,0:T(8,128)(2,1)}) %reduce-scatter.2.cloned.1.call-update) | async-done | bytes 524304 | tf_op jit(solution)/shard_map/reduce_scatter | solution.py:103
  (13 shorter events, 0.0 us)
Async XLA Ops:
  7.4 5.9 %collective-permute-start = (bf16[3,2,1024]{2,1,0:T(2,128)(2,1)S(1)}, bf16[3,2,1024]{2,1,0:T(2,128)(2,1)S(1)}, u32[]{:S(2)}, u32[]{:S(2)}) collective-permute-start(bf16[3,2,1024]{2,1,0:T(2,128)(2,1)S(1)} %slice.69), channel_id=1, source_target_pairs={{0,4},{4,8},{8,12},{12,16},{16,20},{20,24},{24,28},{28,32},{32,36}... | collective-permute-start | bytes 36872 | tf_op jit(solution)/shard_map/ppermute | solution.py:12
  16.1 1.8 copy-start.1
  16.1 1.4 copy-start.4
  16.3 0.8 copy-start.3
  80.4 102.3 %all-to-all-start.1 = ((bf16[4,128,4,1024]{3,2,0,1:T(4,128)(2,1)}), bf16[4,128,4,1024]{3,2,0,1:T(4,128)(2,1)}, u32[]{:S(2)}, u32[]{:S(2)}) async-start(bf16[4,128,4,1024]{3,2,0,1:T(4,128)(2,1)} %copy.35), calls=%async_computation.1 | async-start | bytes 8388608 | tf_op jit(solution)/shard_map/all_to_all | solution.py:67
  86.8 465.1 %reduce-scatter.2.cloned.1.call-start = ((), (), s32[]{:S(2)}) async-start(), calls=%async_computation.7 | async-start | bytes 2621440 | tf_op jit(solution)/shard_map/reduce_scatter | solution.py:103
  217.1 3.0 copy-start
  489.2 25.7 %copy-start.2 = (f32[3,256,1024]{2,1,0:T(8,128)S(1)}, f32[3,256,1024]{2,1,0:T(8,128)}, u32[]{:S(2)}) copy-start(f32[3,256,1024]{2,1,0:T(8,128)} %copy-done.1) | copy-start | bytes 9437188
  489.2 25.7 %copy-start.5 = (f32[1024]{0:T(1024)S(1)}, f32[1024]{0:T(1024)}, u32[]{:S(2)}) copy-start(f32[1024]{0:T(1024)} %param.8) | copy-start | bytes 12292
Sparse Core Ops, SparseCore 0:
  522.6 29.1 reduce-scatter.1
where the time goes:
time: 569 us; the launch traced here: 559 us
  blocking collectives  281 us (49%)
  waiting for transfers between devices  125 us (22%)
  local copies, waits for them, and re-layouts  81.4 us (14%)
  matrix products  34.4 us (6%)
  between operations  14.2 us (2%)
  other arithmetic  11.6 us (2%)
  starting transfers between devices  11.4 us (2%)
    all_to_all x1, blocking collectives, body(): lax.all_to_all(packed, 'ctx', split_axis=2, concat_axis=1, tiled=True)  102 us
    all_to_all x1, waiting for transfers between devices, body(): lax.all_to_all(combined, 'ctx', split_axis=1, concat_axis=2, tiled=True)  95.6 us
    all_to_all x1, blocking collectives, body(): lax.all_to_all(back, 'ctx', split_axis=2, concat_axis=1, tiled=True)  57.1 us
    all_to_all x1, blocking collectives, body(): lax.all_to_all(jnp.stack([prod_real, prod_imag]), 'ctx', split_axis=1, co...  57.1 us
    all_to_all x1, blocking collectives, body(): lax.all_to_all(stacked, 'ctx', split_axis=2, concat_axis=1, tiled=True)  41.8 us
    reduce_scatter x1, waiting for transfers between devices, body(): lax.psum_scatter(terms.astype(jnp.bfloat16), 'tp', scatter_dimension=1, t...  29.3 us
    all_to_all x1, blocking collectives, body(): lax.all_to_all(conv_rows, 'ctx', split_axis=0, concat_axis=1, tiled=True)  23.2 us
    unnamed x16, local copies, waits for them, and re-layouts  12.4 us
  transfers between devices with their start and end apart: 3, of which 2 were waited for; matrix products, arithmetic and copies ran while one was open for 0% of the time, Pallas kernels for 0%

commit v1 on v0

v1 whole, which is shorter than its diff:
```python
import functools

import jax
import jax.numpy as jnp
import numpy as np
from jax import lax
from jax.experimental import pallas as pl
from jax.experimental.pallas import tpu as pltpu
from jax.sharding import PartitionSpec as P

GROUP = 13


def tables(blocks, width, lanes):
    freqs = blocks + 1
    points = 2 * blocks * width
    f = np.arange(freqs)
    angle = 2.0 * np.pi * np.outer(f, np.arange(blocks)) / (2 * blocks)
    steps = freqs // GROUP
    eye = np.eye(lanes)
    pair = np.stack([np.cos(angle), -np.sin(angle)]).reshape(2, steps, GROUP, blocks)
    pair = pair.transpose(1, 0, 2, 3).reshape(2 * freqs, blocks)
    lead = np.kron(pair, eye)
    weight = np.where((f == 0) | (f == blocks), 1.0, 2.0)[:, None] / points
    turn = 2.0 * np.pi * np.outer(f, np.arange(width)) / points
    twiddle = np.stack([np.cos(turn), -np.sin(turn)])
    twiddle = np.repeat(twiddle, lanes, axis=1)
    inner = 2.0 * np.pi * np.outer(np.arange(width), np.arange(width)) / width
    c, s = np.cos(inner), np.sin(inner)
    forward = np.block([[c, -s], [s, c]])
    backward = np.block([[c, s], [-s, c]])
    scaled = np.stack([np.cos(angle) * weight, -np.sin(angle) * weight]).reshape(2, steps, GROUP, blocks)
    scaled = scaled.transpose(1, 0, 2, 3).reshape(2 * freqs, blocks)
    tail = np.kron(scaled.T, eye)
    half = jnp.bfloat16
    return (
        lead.astype(half),
        tail.astype(half),
        twiddle.astype(np.float32),
        forward.astype(half),
        backward.astype(half),
    )


def dot(left, right):
    return jnp.dot(left, right, preferred_element_type=jnp.float32)


def conv_kernel(x_ref, h_ref, lead_ref, tail_ref, twiddle_ref, forward_ref, backward_ref, y_ref, back_ref, rows, steps):
    width = x_ref.shape[1]

    def step(i, carry):
        at = pl.ds(pl.multiple_of(i * rows, 16), rows)
        at2 = pl.ds(pl.multiple_of(i * 2 * rows, 16), 2 * rows)
        cos = twiddle_ref[0, at, :]
        sin = twiddle_ref[1, at, :]

        def spectrum(ref):
            first = dot(lead_ref[at2, :], ref[...])
            real, imag = first[:rows], first[rows:]
            turned = jnp.concatenate([real * cos - imag * sin, real * sin + imag * cos], axis=1)
            return dot(turned.astype(jnp.bfloat16), forward_ref[...])

        sx = spectrum(x_ref)
        sh = spectrum(h_ref)
        xr, xi = sx[:, :width], sx[:, width:]
        hr, hi = sh[:, :width], sh[:, width:]
        product = jnp.concatenate([xr * hr - xi * hi, xr * hi + xi * hr], axis=1)
        back = dot(product.astype(jnp.bfloat16), backward_ref[...])
        br, bi = back[:, :width], back[:, width:]
        out = jnp.concatenate([br * cos + bi * sin, bi * cos - br * sin], axis=0)
        back_ref[at2, :] = out.astype(jnp.bfloat16)
        return carry

    lax.fori_loop(0, steps, step, 0)
    y_ref[...] = dot(tail_ref[...], back_ref[...]).astype(jnp.bfloat16)


def long_conv(x, h):
    blocks, lanes, width = x.shape
    consts = tables(blocks, width, lanes)
    freqs = blocks + 1
    vmem = pl.BlockSpec(memory_space=pltpu.VMEM)
    out = pl.pallas_call(
        functools.partial(conv_kernel, rows=GROUP * lanes, steps=freqs // GROUP),
        out_shape=jax.ShapeDtypeStruct((blocks * lanes, width), jnp.bfloat16),
        in_specs=[vmem] * 7,
        out_specs=vmem,
        scratch_shapes=[pltpu.VMEM((2 * freqs * lanes, width), jnp.bfloat16)],
        compiler_params=pltpu.CompilerParams(vmem_limit_bytes=48 << 20),
    )(x.reshape(blocks * lanes, width), h.reshape(blocks * lanes, width), *[jnp.asarray(c) for c in consts])
    return out.reshape(blocks, lanes, width)


def body(qkv, short_taps, long_filter, skip, out_weight):
    f32 = jnp.float32
    blocks = lax.axis_size("ctx")
    tokens, channels = qkv.shape[1:]
    lanes = channels // blocks
    edge = lax.ppermute(qkv[:, tokens - 2 :, :], "ctx", [(i, i + 1) for i in range(blocks - 1)])
    padded = jnp.concatenate([edge, qkv], axis=1).astype(f32)
    shortened = (
        short_taps[:, 0][:, None, :] * padded[:, 2:]
        + short_taps[:, 1][:, None, :] * padded[:, 1:-1]
        + short_taps[:, 2][:, None, :] * padded[:, :-2]
    )
    signal = (shortened[1] * shortened[2]).astype(jnp.bfloat16)

    def exchange(value):
        return lax.all_to_all(value.reshape(blocks, lanes, tokens), "ctx", split_axis=0, concat_axis=0, tiled=True)

    taps = exchange(long_filter.T)
    spread = exchange(signal.T)
    conv = exchange(long_conv(spread, taps)).reshape(channels, tokens).T
    gated = (shortened[0] * (conv.astype(f32) + skip * signal.astype(f32))).astype(jnp.bfloat16)
    terms = jnp.dot(gated, out_weight, preferred_element_type=f32)
    return lax.psum_scatter(terms.astype(jnp.bfloat16), "tp", scatter_dimension=1, tiled=True)


def solution(mesh):
    placed = (P(None, "ctx", "tp"), P(None, None, "tp"), P("ctx", "tp"), P("tp"), P("tp", None))
    return jax.shard_map(body, mesh=mesh, in_specs=placed, out_specs=P("ctx", "tp"), check_vma=False)
```

time: 569 us -> 149 us (0.26); the launches traced: 559 us -> 148 us
  blocking collectives: 281 us -> 47 us
  waiting for transfers between devices: 125 us -> 36.8 us
  local copies, waits for them, and re-layouts: 81.4 us -> 8.65 us
  matrix products: 34.4 us -> 7.25 us
  Pallas kernels: 0 us -> 14.1 us
  other arithmetic: 11.6 us -> 5.03 us
    all_to_all x5 -> x2, blocking collectives: 281 us -> 47 us  [exchange(): lax.all_to_all(value.reshape(blocks, lanes, tokens), 'ctx', split_axis=0,...]
    all_to_all x1, waiting for transfers between devices: 95.6 us -> 7.46 us  [exchange(): lax.all_to_all(value.reshape(blocks, lanes, tokens), 'ctx', split_axis=0,...]
    dot_general x12 -> x0, matrix products: 26.8 us -> none  [the longest x1 4.12 us: body(): jnp.einsum('lkj,sljc->slkc', col_cos, part_imag, preferred_element_type=f32)]
    all_to_all x4 -> x0, local copies, waits for them, and re-layouts: 18.2 us -> none  [the longest x1 10.6 us: body(): lax.all_to_all(combined, 'ctx', split_axis=1, concat_axis=2, tiled=True)]
    another operation x4 -> x0, local copies, waits for them, and re-layouts: 16.4 us -> none  [the longest x1 6.72 us: body(): jnp.stack([spec_real, spec_imag], axis=1).reshape(4, 2, tok_rows, channels)]
    pallas_call x0 -> x1, Pallas kernels: none -> 14.1 us  [long_conv(): pl.pallas_call(functools.partial(conv_kernel, rows=GROUP * lanes, steps=f...]
    slice x6 -> x1, local copies, waits for them, and re-layouts: 12.5 us -> 0.81 us  [body(): qkv[:, tokens - 2:, :]]
    convert_element_type x3 -> x0, local copies, waits for them, and re-layouts: 9.87 us -> none  [the longest x1 7.38 us: body(): combined = jnp.stack([first_real, first_imag], axis=1).astype(jnp.bfloat16)]
  transfers between devices with their start and end apart: 3 -> 3, of which waited for: 2 -> 2; matrix products, arithmetic and copies ran while one was open for 0% -> 7% of each run, Pallas kernels for 0% -> 0%
where the time goes in v1:
time: 149 us; the launch traced here: 148 us
  blocking collectives  47 us (32%)
  waiting for transfers between devices  36.8 us (25%)
  starting transfers between devices  15.8 us (11%)
  Pallas kernels  14.1 us (9%)
  between operations  13.5 us (9%)
  local copies, waits for them, and re-layouts  8.65 us (6%)
  matrix products  7.25 us (5%)
  other arithmetic  5.03 us (3%)
    all_to_all x2, blocking collectives, exchange(): lax.all_to_all(value.reshape(blocks, lanes, tokens), 'ctx', split_axis=0,...  47 us
    reduce_scatter x1, waiting for transfers between devices, body(): lax.psum_scatter(terms.astype(jnp.bfloat16), 'tp', scatter_dimension=1, t...  29.3 us
    pallas_call x1, Pallas kernels, long_conv(): pl.pallas_call(functools.partial(conv_kernel, rows=GROUP * lanes, steps=f...  14.1 us
    all_to_all x1, starting transfers between devices, exchange(): lax.all_to_all(value.reshape(blocks, lanes, tokens), 'ctx', split_axis=0,...  10.9 us
    all_to_all x1, waiting for transfers between devices, exchange(): lax.all_to_all(value.reshape(blocks, lanes, tokens), 'ctx', split_axis=0,...  7.46 us
    dot_general x1, matrix products, body(): terms = jnp.dot(gated, out_weight, preferred_element_type=f32)  7.25 us
    unnamed x18, local copies, waits for them, and re-layouts  6.47 us
    ppermute x1, starting transfers between devices, body(): lax.ppermute(qkv[:, tokens - 2:, :], 'ctx', [(i, i + 1) for i in range(bl...  4.94 us
  transfers between devices with their start and end apart: 3, of which 2 were waited for; matrix products, arithmetic and copies ran while one was open for 7% of the time, Pallas kernels for 0%

profile of v1, /device:TPU:1, one launch (start us, length us, event | category | flops | bytes accessed | tf_op | source)
XLA Modules:
  0.0 148.2 jit_solution(932932427486206782)
XLA Ops:
  6.5 0.8 slice.31
  7.4 4.9 %collective-permute-start = (bf16[3,2,1024]{2,1,0:T(2,128)(2,1)S(1)}, bf16[3,2,1024]{2,1,0:T(2,128)(2,1)S(1)}, u32[]{:S(2)}, u32[]{:S(2)}) collective-permute-start(bf16[3,2,1024]{2,1,0:T(2,128)(2,1)S(1)} %slice.31), channel_id=1, source_target_pairs={{0,4},{4,8},{8,12},{12,16},{16,20},{20,24},{24,28},{28,32},{32,36}... | collective-permute-start | bytes 36872 | tf_op jit(solution)/shard_map/ppermute | solution.py:100
  12.3 2.1 %copy.19 = bf16[256,1024]{0,1:T(8,128)(2,1)} copy(bf16[256,1024]{1,0:T(8,128)(2,1)} %param.12) | data formatting | bytes 1048576 | tf_op args[2]
  14.4 10.9 %all-to-all-start.1 = ((bf16[64,16,256]{2,1,0:T(8,128)(2,1)}), bf16[64,16,256]{2,1,0:T(8,128)(2,1)S(1)}, u32[]{:S(2)}, u32[]{:S(2)}) async-start(bf16[64,16,256]{2,1,0:T(8,128)(2,1)} %bitcast.6), calls=%async_computation.1 | async-start | bytes 1048576 | tf_op jit(solution)/shard_map/all_to_all | solution.py:110
  25.2 0.0 reduce-scatter.2.cloned.1.call-start
  25.3 0.9 fusion.9
  26.3 1.7 %copy.18 = bf16[3,256,1024]{1,2,0:T(8,128)(2,1)S(1)} copy(bf16[3,256,1024]{2,1,0:T(8,128)(2,1)} %param.10) | data formatting | bytes 3145728 | tf_op args[0]
  28.0 0.0 collective-permute-done
  28.0 0.4 copy.17
  28.4 1.0 maximum_convert_fusion
  29.4 3.2 %fusion = f32[3,256,1024]{1,2,0:T(8,128)S(1)} fusion(f32[3,258,1024]{1,2,0:T(8,128)S(1)} %maximum_convert_fusion, f32[3,1024]{1,0:T(4,128)S(1)} %get-tuple-element.8, f32[3,1024]{1,0:T(4,128)S(1)} %get-tuple-element.9, f32[3,1024]{1,0:T(4,128)S(1)} %bitcast.44), kind=kLoop, calls=%fused_computation.2 | loop fusion | flops 3932160 | bytes 12619776 | tf_op jit(solution)/shard_map/add | solution.py:103
  32.6 0.0 copy-start.3
  32.6 1.6 %copy-done.3 = f32[3,256,1024]{1,2,0:T(8,128)} copy-done((f32[3,256,1024]{1,2,0:T(8,128)}, f32[3,256,1024]{1,2,0:T(8,128)S(1)}, u32[]{:S(2)}) %copy-start.3) | copy-done | bytes 3145752
  34.2 0.0 copy-start
  34.2 0.0 copy-start.1
  34.2 0.9 fusion.2
  35.1 7.5 %all-to-all-done.1 = bf16[64,16,256]{2,1,0:T(8,128)(2,1)S(1)} async-done(((bf16[64,16,256]{2,1,0:T(8,128)(2,1)}), bf16[64,16,256]{2,1,0:T(8,128)(2,1)S(1)}, u32[]{:S(2)}, u32[]{:S(2)}) %all-to-all-start.1) | async-done | bytes 524320 | tf_op jit(solution)/shard_map/all_to_all | solution.py:110
  42.6 23.6 %all_to_all.15 = bf16[64,16,256]{2,1,0:T(8,128)(2,1)S(1)} all-to-all(bf16[64,16,256]{2,1,0:T(8,128)(2,1)} %bitcast.42), channel_id=1, replica_groups=mesh['ctx'=64,'tp'=4] {'ctx'}, dimensions={0} | all-to-all | bytes 1048576 | tf_op jit(solution)/shard_map/all_to_all | solution.py:110
  66.2 0.0 copy-done
  66.2 0.0 copy-done.1
  66.2 0.0 copy-start.2
  66.2 1.0 copy-done.2
  67.2 0.0 copy-start.4
  67.2 0.0 copy-start.5
  67.2 0.0 copy-start.6
  67.2 14.1 %shard_map.100 = bf16[1024,256]{1,0:T(8,128)(2,1)S(1)} custom-call(bf16[1024,256]{1,0:T(8,128)(2,1)S(1)} %bitcast.41, bf16[1024,256]{1,0:T(8,128)(2,1)S(1)} %bitcast.39, bf16[2080,1024]{1,0:T(8,128)(2,1)} %constant.10.clone.lead_ref, bf16[1024,2080]{1,0:T(8,128)(2,1)} %constant.11.clone.tail_ref, f32[2,1040,256]{2,1,0:T(8,128)S(1)} %copy-done, ...), custom_call_target="tpu_custom_call" | custom-call | tf_op jit(solution)/shard_map/pallas_call | solution.py:84
  81.3 23.4 %all_to_all.16 = bf16[64,16,256]{2,1,0:T(8,128)(2,1)S(1)} all-to-all(bf16[64,16,256]{2,1,0:T(8,128)(2,1)S(1)} %bitcast.40), channel_id=1, replica_groups=mesh['ctx'=64,'tp'=4] {'ctx'}, dimensions={0} | all-to-all | bytes 1048576 | tf_op jit(solution)/shard_map/all_to_all | solution.py:110
  104.7 0.0 copy-done.4
  104.7 0.0 copy-done.5
  104.7 0.0 copy-done.6
  104.7 7.2 %convolution_convert_fusion = bf16[256,4096]{1,0:T(8,128)(2,1)} fusion(bf16[1024,4096]{1,0:T(8,128)(2,1)} %param.14, f32[3,256,1024]{1,2,0:T(8,128)S(1)} %copy-done.4, bf16[1024,256]{1,0:T(8,128)(2,1)S(1)} %bitcast.43, bf16[1,256,1024]{1,2,0:T(8,128)(2,1)S(1)} %copy-done.5, f32[1024]{0:T(1024)S(1)} %copy-done.6), kind=kOutput, calls=%fused_computation | convolution fusion | flops 2150105088 | bytes 12587008 | tf_op jit(solution)/shard_map/dot_general | solution.py:116
  112.0 0.0 reduce-scatter.2.cloned.1.call-update
  112.0 29.3 %reduce-scatter.2.cloned.1.call-done = bf16[256,1024]{1,0:T(8,128)(2,1)} async-done(((bf16[256,4096]{1,0:T(8,128)(2,1)}), bf16[256,1024]{1,0:T(8,128)(2,1)}) %reduce-scatter.2.cloned.1.call-update) | async-done | bytes 524304 | tf_op jit(solution)/shard_map/reduce_scatter | solution.py:117
  (2 shorter events, 0.0 us)
Async XLA Ops:
  7.4 20.6 %collective-permute-start = (bf16[3,2,1024]{2,1,0:T(2,128)(2,1)S(1)}, bf16[3,2,1024]{2,1,0:T(2,128)(2,1)S(1)}, u32[]{:S(2)}, u32[]{:S(2)}) collective-permute-start(bf16[3,2,1024]{2,1,0:T(2,128)(2,1)S(1)} %slice.31), channel_id=1, source_target_pairs={{0,4},{4,8},{8,12},{12,16},{16,20},{20,24},{24,28},{28,32},{32,36}... | collective-permute-start | bytes 36872 | tf_op jit(solution)/shard_map/ppermute | solution.py:100
  14.4 28.2 %all-to-all-start.1 = ((bf16[64,16,256]{2,1,0:T(8,128)(2,1)}), bf16[64,16,256]{2,1,0:T(8,128)(2,1)S(1)}, u32[]{:S(2)}, u32[]{:S(2)}) async-start(bf16[64,16,256]{2,1,0:T(8,128)(2,1)} %bitcast.6), calls=%async_computation.1 | async-start | bytes 1048576 | tf_op jit(solution)/shard_map/all_to_all | solution.py:110
  25.2 116.1 %reduce-scatter.2.cloned.1.call-start = ((), (), s32[]{:S(2)}) async-start(), calls=%async_computation.4 | async-start | bytes 2621440 | tf_op jit(solution)/shard_map/reduce_scatter | solution.py:117
  32.6 1.6 %copy-start.3 = (f32[3,256,1024]{1,2,0:T(8,128)}, f32[3,256,1024]{1,2,0:T(8,128)S(1)}, u32[]{:S(2)}) copy-start(f32[3,256,1024]{1,2,0:T(8,128)S(1)} %fusion) | copy-start | bytes 9437188
  34.2 32.0 %copy-start = (f32[2,1040,256]{2,1,0:T(8,128)S(1)}, f32[2,1040,256]{2,1,0:T(8,128)}, u32[]{:S(2)}) copy-start(f32[2,1040,256]{2,1,0:T(8,128)} %constant.12.clone.twiddle_ref) | copy-start | bytes 6389764
  34.2 32.0 %copy-start.1 = (bf16[512,512]{1,0:T(8,128)(2,1)S(1)}, bf16[512,512]{1,0:T(8,128)(2,1)}, u32[]{:S(2)}) copy-start(bf16[512,512]{1,0:T(8,128)(2,1)} %constant.13.clone.forward_ref) | copy-start | bytes 1572868
  66.2 1.0 copy-start.2
  67.2 37.5 %copy-start.4 = (f32[3,256,1024]{1,2,0:T(8,128)S(1)}, f32[3,256,1024]{1,2,0:T(8,128)}, u32[]{:S(2)}) copy-start(f32[3,256,1024]{1,2,0:T(8,128)} %copy-done.3) | copy-start | bytes 9437188
  67.2 37.5 %copy-start.5 = (bf16[1,256,1024]{1,2,0:T(8,128)(2,1)S(1)}, bf16[1,256,1024]{1,2,0:T(8,128)(2,1)}, u32[]{:S(2)}) copy-start(bf16[1,256,1024]{1,2,0:T(8,128)(2,1)} %fusion.2) | copy-start | bytes 1572868
  67.2 37.5 %copy-start.6 = (f32[1024]{0:T(1024)S(1)}, f32[1024]{0:T(1024)}, u32[]{:S(2)}) copy-start(f32[1024]{0:T(1024)} %param.13) | copy-start | bytes 12292
Sparse Core Ops, SparseCore 0:
  112.1 29.1 reduce-scatter.1

commit v2 on v1

v2 whole, which is shorter than its diff:
```python
import functools

import jax
import jax.numpy as jnp
import numpy as np
from jax import lax
from jax.experimental import pallas as pl
from jax.experimental.pallas import tpu as pltpu
from jax.sharding import PartitionSpec as P

MESH = pl.DeviceIdType.MESH
GROUP = 13
LANE = 128
HALO = 16


def tables(blocks, width, lanes):
    freqs = blocks + 1
    points = 2 * blocks * width
    f = np.arange(freqs)
    angle = 2.0 * np.pi * np.outer(f, np.arange(blocks)) / (2 * blocks)
    steps = freqs // GROUP
    eye = np.eye(lanes)
    pair = np.stack([np.cos(angle), -np.sin(angle)]).reshape(2, steps, GROUP, blocks)
    pair = pair.transpose(1, 0, 2, 3).reshape(2 * freqs, blocks)
    lead = np.kron(pair, eye)
    weight = np.where((f == 0) | (f == blocks), 1.0, 2.0)[:, None] / points
    turn = 2.0 * np.pi * np.outer(f, np.arange(width)) / points
    twiddle = np.stack([np.cos(turn), -np.sin(turn)])
    twiddle = np.repeat(twiddle, lanes, axis=1)
    inner = 2.0 * np.pi * np.outer(np.arange(width), np.arange(width)) / width
    c, s = np.cos(inner), np.sin(inner)
    forward = np.block([[c, -s], [s, c]])
    backward = np.block([[c, s], [-s, c]])
    scaled = np.stack([np.cos(angle) * weight, -np.sin(angle) * weight]).reshape(2, steps, GROUP, blocks)
    scaled = scaled.transpose(1, 0, 2, 3).reshape(2 * freqs, blocks)
    tail = np.kron(scaled.T, eye)
    half = jnp.bfloat16
    return (
        lead.astype(half),
        tail.astype(half),
        twiddle.astype(np.float32),
        forward.astype(half),
        backward.astype(half),
    )


def dot(left, right):
    return jnp.dot(left, right, preferred_element_type=jnp.float32)


def kernel(
    blocks,
    tps,
    lanes,
    qkv_hbm,
    taps_ref,
    filter_hbm,
    skip_ref,
    weight_hbm,
    lead_hbm,
    tail_hbm,
    twiddle_hbm,
    forward_hbm,
    backward_hbm,
    out_ref,
    qkv_ref,
    filter_ref,
    weight_ref,
    lead_ref,
    tail_ref,
    twiddle_ref,
    forward_ref,
    backward_ref,
    halo_ref,
    filter_t,
    signal_t,
    signal_ref,
    query_ref,
    h_ref,
    x_ref,
    sh_ref,
    back_ref,
    y_ref,
    conv_ref,
    gated_ref,
    relay_src,
    relay_in,
    part_ref,
    send_ref,
    take_ref,
    load_sem,
    halo_sem,
    filter_sem,
    signal_sem,
    conv_send,
    conv_recv,
    tp_send,
    tp_recv,
):
    f32 = jnp.float32
    bf16 = jnp.bfloat16
    me = lax.axis_index("ctx")
    col = lax.axis_index("tp")
    tokens, channels = filter_ref.shape
    half_tok = tokens // 2
    half_col = out_ref.shape[1] // 2
    cols = out_ref.shape[1]

    sources = (filter_hbm, qkv_hbm, lead_hbm, twiddle_hbm, forward_hbm, weight_hbm, backward_hbm, tail_hbm)
    targets = (filter_ref, qkv_ref, lead_ref, twiddle_ref, forward_ref, weight_ref, backward_ref, tail_ref)
    loads = [pltpu.make_async_copy(s, t, load_sem.at[i]) for i, (s, t) in enumerate(zip(sources, targets))]
    for load in loads:
        load.start()

    barrier = pltpu.get_barrier_semaphore()

    def greet(i, carry):
        pl.semaphore_signal(barrier, inc=1, device_id={"ctx": lax.rem(me + i, blocks)}, device_id_type=MESH)
        return carry

    lax.fori_loop(1, blocks, greet, 0)
    right = lax.rem(col + 1, tps)
    left = lax.rem(col + tps - 1, tps)
    for side in (left, right):
        pl.semaphore_signal(barrier, inc=1, device_id={"tp": side}, device_id_type=MESH)

    per = LANE // lanes
    chunks = channels // LANE

    def piece(ref, p):
        return ref.at[pl.ds(pl.multiple_of(p * lanes, lanes), lanes)]

    def chunk_at(i):
        return pl.ds(pl.multiple_of(i * LANE, LANE), LANE)

    def scatter(src, dst, sems, chunk):
        def one(k, carry):
            p = chunk * per + lax.rem(me + k, per)

            @pl.when(p != me)
            def _():
                pltpu.make_async_remote_copy(
                    piece(src, p), piece(dst, me), sems.at[0], sems.at[1], device_id={"ctx": p}, device_id_type=MESH
                ).start()

            return carry

        lax.fori_loop(0, per, one, 0)

    def settled(src, dst, sems):
        rows = (blocks - 1) * lanes
        return pltpu.make_async_remote_copy(
            src.at[pl.ds(0, rows)],
            dst.at[pl.ds(0, rows)],
            sems.at[0],
            sems.at[1],
            device_id={"ctx": me},
            device_id_type=MESH,
        )

    own = pl.ds(pl.multiple_of(me * lanes, lanes), lanes)

    loads[0].wait()

    def flip(i, carry):
        at = chunk_at(i)
        filter_t[at, :] = filter_ref[:, at].astype(f32).T.astype(bf16)
        return carry

    lax.fori_loop(0, chunks, flip, 0)
    loads[1].wait()
    pl.semaphore_wait(barrier, blocks + 1)

    halo = pltpu.make_async_remote_copy(
        qkv_ref.at[:, pl.ds(tokens - HALO, HALO)],
        halo_ref,
        halo_sem.at[0],
        halo_sem.at[1],
        device_id={"ctx": lax.rem(me + 1, blocks)},
        device_id_type=MESH,
    )
    halo.start()

    def send_filter(i, carry):
        scatter(filter_t, h_ref, filter_sem, lax.rem(me // per + i, chunks))
        return carry

    lax.fori_loop(0, chunks, send_filter, 0)
    h_ref[own, :] = filter_t[own, :]
    halo.wait()

    def shortened(i, at):
        edge = jnp.where(me > 0, halo_ref[i, :, at].astype(f32), 0.0)
        wide = jnp.concatenate([edge, qkv_ref[i, :, at].astype(f32)], axis=0)
        return (
            taps_ref[i, 0:1, at] * wide[HALO:]
            + taps_ref[i, 1:2, at] * wide[HALO - 1 : HALO - 1 + tokens]
            + taps_ref[i, 2:3, at] * wide[HALO - 2 : HALO - 2 + tokens]
        )

    def send_signal(i, carry):
        chunk = lax.rem(me // per + i, chunks)
        at = chunk_at(chunk)
        signal = (shortened(1, at) * shortened(2, at)).astype(bf16)
        signal_ref[:, at] = signal
        signal_t[at, :] = signal.astype(f32).T.astype(bf16)
        scatter(signal_t, x_ref, signal_sem, chunk)
        return carry

    lax.fori_loop(0, chunks, send_signal, 0)
    x_ref[own, :] = signal_t[own, :]

    def query(i, carry):
        at = chunk_at(i)
        query_ref[:, at] = shortened(0, at)
        return carry

    lax.fori_loop(0, chunks, query, 0)

    width = tokens
    rows = GROUP * lanes
    steps = (blocks + 1) // GROUP

    def tables_at(i):
        at = pl.ds(pl.multiple_of(i * rows, 16), rows)
        at2 = pl.ds(pl.multiple_of(i * 2 * rows, 16), 2 * rows)
        return at, at2, twiddle_ref[0, at, :], twiddle_ref[1, at, :]

    def spectrum(ref, i):
        _, at2, cos, sin = tables_at(i)
        first = dot(lead_ref[at2, :], ref[...])
        real, imag = first[:rows], first[rows:]
        turned = jnp.concatenate([real * cos - imag * sin, real * sin + imag * cos], axis=1)
        return dot(turned.astype(bf16), forward_ref[...])

    for load in loads[2:5]:
        load.wait()
    from_filter = settled(filter_t, h_ref, filter_sem)
    from_filter.wait_recv()

    def filter_step(i, carry):
        at = tables_at(i)[0]
        sh_ref[at, :] = spectrum(h_ref, i).astype(bf16)
        return carry

    lax.fori_loop(0, steps, filter_step, 0)
    for load in loads[5:]:
        load.wait()
    from_filter.wait_send()
    from_signal = settled(signal_t, x_ref, signal_sem)
    from_signal.wait_recv()

    def signal_step(i, carry):
        at, at2, cos, sin = tables_at(i)
        sx = spectrum(x_ref, i)
        xr, xi = sx[:, :width], sx[:, width:]
        hr, hi = sh_ref[at, :width].astype(f32), sh_ref[at, width:].astype(f32)
        product = jnp.concatenate([xr * hr - xi * hi, xr * hi + xi * hr], axis=1)
        back = dot(product.astype(bf16), backward_ref[...])
        br, bi = back[:, :width], back[:, width:]
        out = jnp.concatenate([br * cos + bi * sin, bi * cos - br * sin], axis=0)
        back_ref[at2, :] = out.astype(bf16)
        return carry

    lax.fori_loop(0, steps, signal_step, 0)

    group = 16
    big = group * lanes
    turns = blocks // group

    def send_conv(i, h):
        first = lax.rem(me // group + i, turns) * group

        def one(k, carry):
            p = first + lax.rem(me + k, group)

            @pl.when(p != me)
            def _():
                pltpu.make_async_remote_copy(
                    piece(y_ref.at[h], p),
                    piece(conv_ref.at[h], me),
                    conv_send.at[h],
                    conv_recv.at[h],
                    device_id={"ctx": p},
                    device_id_type=MESH,
                ).start()

            return carry

        lax.fori_loop(0, group, one, 0)

    def last_step(i, carry):
        at = pl.ds(pl.multiple_of(lax.rem(me // group + i, turns) * big, 16), big)
        y = dot(tail_ref[at, :], back_ref[...]).astype(bf16)
        y_ref[0, at, :] = y[:, :half_tok]
        y_ref[1, at, :] = y[:, half_tok:]
        send_conv(i, 0)
        return carry

    lax.fori_loop(0, turns, last_step, 0)

    def rest_step(i, carry):
        send_conv(i, 1)
        return carry

    lax.fori_loop(0, turns, rest_step, 0)
    from_conv = []
    for h in range(2):
        conv_ref[h, own, :] = y_ref[h, own, :]
        rows_all = pl.ds(0, (blocks - 1) * lanes)
        from_conv.append(
            pltpu.make_async_remote_copy(
                y_ref.at[h, rows_all],
                conv_ref.at[h, rows_all],
                conv_send.at[h],
                conv_recv.at[h],
                device_id={"ctx": me},
                device_id_type=MESH,
            )
        )

    def tp_copy(src, dst, h, kind, side):
        s = (h * 3 + kind) * 2 + side
        return pltpu.make_async_remote_copy(
            src, dst, tp_send.at[s], tp_recv.at[s], device_id={"tp": (right, left)[side]}, device_id_type=MESH
        )

    def product(h, dest, start):
        at = pl.ds(pl.multiple_of(dest * cols + start, half_col), half_col)
        return dot(gated_ref[h], weight_ref[:, at])

    far = lax.rem(col + 2, tps)
    relays, opens, sums = [], [], []
    for h in range(2):
        from_conv[h].wait_recv()
        tok = pl.ds(h * half_tok, half_tok)

        def gate(i, carry):
            at = chunk_at(i)
            conv = conv_ref[h, at, :].astype(f32).T
            signal = signal_ref[tok, at].astype(f32)
            gated_ref[h, :, at] = (query_ref[tok, at] * (conv + skip_ref[:, at] * signal)).astype(bf16)
            return carry

        lax.fori_loop(0, chunks, gate, 0)
        for side in range(2):
            relay_src[h, side] = product(h, far, side * half_col).astype(bf16)
            copy = tp_copy(relay_src.at[h, side], relay_in.at[h, side], h, 0, side)
            copy.start()
            relays.append(copy)
        for side, dest in ((0, right), (1, left)):
            send_ref[h, side, 1] = product(h, dest, (1 - side) * half_col).astype(bf16)
            copy = tp_copy(send_ref.at[h, side, 1], take_ref.at[h, side, 1], h, 1, side)
            copy.start()
            opens.append(copy)
        for side, dest in ((0, right), (1, left)):
            part_ref[side] = product(h, dest, side * half_col)
        for side in range(2):
            relays[2 * h + side].wait_recv()
            send_ref[h, side, 0] = (part_ref[side] + relay_in[h, side].astype(f32)).astype(bf16)
            copy = tp_copy(send_ref.at[h, side, 0], take_ref.at[h, side, 0], h, 2, side)
            copy.start()
            sums.append(copy)
        for part in range(2):
            part_ref[2 + 2 * h + part] = product(h, col, part * half_col)

    for h in range(2):
        for side in range(2):
            opens[2 * h + side].wait_recv()
            sums[2 * h + side].wait_recv()
        tok = pl.ds(h * half_tok, half_tok)
        for part in range(2):
            total = (
                part_ref[2 + 2 * h + part]
                + take_ref[h, 0, part].astype(f32)
                + take_ref[h, 1, 1 - part].astype(f32)
            )
            out_ref[tok, pl.ds(part * half_col, half_col)] = total.astype(bf16)

    from_signal.wait_send()
    for copy in from_conv + relays + opens + sums:
        copy.wait_send()


def body(qkv, short_taps, long_filter, skip, out_weight):
    blocks = lax.axis_size("ctx")
    tps = lax.axis_size("tp")
    tokens, channels = qkv.shape[1:]
    lanes = channels // blocks
    cols = out_weight.shape[1] // tps
    consts = [jnp.asarray(c) for c in tables(blocks, tokens, lanes)]
    freqs = (blocks + 1) * lanes
    vmem = pl.BlockSpec(memory_space=pltpu.VMEM)
    hbm = pl.BlockSpec(memory_space=pl.ANY)
    bf16 = jnp.bfloat16
    f32 = jnp.float32
    dma = pltpu.SemaphoreType.DMA
    half = tokens // 2
    return pl.pallas_call(
        functools.partial(kernel, blocks, tps, lanes),
        out_shape=jax.ShapeDtypeStruct((tokens, cols), bf16),
        in_specs=[hbm, vmem, hbm, vmem] + [hbm] * 6,
        out_specs=vmem,
        scratch_shapes=[
            pltpu.VMEM(qkv.shape, bf16),
            pltpu.VMEM((tokens, channels), bf16),
            pltpu.VMEM(out_weight.shape, bf16),
            *[pltpu.VMEM(c.shape, c.dtype) for c in consts],
            pltpu.VMEM((3, HALO, channels), bf16),
            pltpu.VMEM((channels, tokens), bf16),
            pltpu.VMEM((channels, tokens), bf16),
            pltpu.VMEM((tokens, channels), bf16),
            pltpu.VMEM((tokens, channels), f32),
            pltpu.VMEM((channels, tokens), bf16),
            pltpu.VMEM((channels, tokens), bf16),
            pltpu.VMEM((freqs, 2 * tokens), bf16),
            pltpu.VMEM((2 * freqs, tokens), bf16),
            pltpu.VMEM((2, channels, half), bf16),
            pltpu.VMEM((2, channels, half), bf16),
            pltpu.VMEM((2, half, channels), bf16),
            pltpu.VMEM((2, 2, half, cols // 2), bf16),
            pltpu.VMEM((2, 2, half, cols // 2), bf16),
            pltpu.VMEM((6, half, cols // 2), f32),
            pltpu.VMEM((2, 2, 2, half, cols // 2), bf16),
            pltpu.VMEM((2, 2, 2, half, cols // 2), bf16),
            dma((8,)),
            dma((2,)),
            dma((2,)),
            dma((2,)),
            dma((2,)),
            dma((2,)),
            dma((12,)),
            dma((12,)),
        ],
        compiler_params=pltpu.CompilerParams(
            collective_id=0, has_side_effects=True, vmem_limit_bytes=56 << 20
        ),
        name="hyena",
    )(qkv, short_taps, long_filter, skip[None, :], out_weight, *consts)


def solution(mesh):
    placed = (P(None, "ctx", "tp"), P(None, None, "tp"), P("ctx", "tp"), P("tp"), P("tp", None))
    return jax.shard_map(body, mesh=mesh, in_specs=placed, out_specs=P("ctx", "tp"), check_vma=False)
```

time: 149 us -> 79.8 us (0.54)
  Pallas kernels: 14.1 us -> 77.7 us
  blocking collectives: 47 us -> 0 us
  waiting for transfers between devices: 36.8 us -> 0 us
  starting transfers between devices: 15.8 us -> 0 us
  between operations: 13.5 us -> 0.01 us
  matrix products: 7.25 us -> 0 us
  local copies, waits for them, and re-layouts: 8.65 us -> 1.87 us
  other arithmetic: 5.03 us -> 0 us
    pallas_call x1, Pallas kernels: 14.1 us -> 77.7 us  [body(): pl.pallas_call(functools.partial(kernel, blocks, tps, lanes), out_shape=j...]
    all_to_all x2 -> x0, blocking collectives: 47 us -> none  [exchange(): lax.all_to_all(value.reshape(blocks, lanes, tokens), 'ctx', split_axis=0,...]
    reduce_scatter x1 -> x0, waiting for transfers between devices: 29.3 us -> none  [body(): lax.psum_scatter(terms.astype(jnp.bfloat16), 'tp', scatter_dimension=1, t...]
    all_to_all x1 -> x0, starting transfers between devices: 10.9 us -> none  [exchange(): lax.all_to_all(value.reshape(blocks, lanes, tokens), 'ctx', split_axis=0,...]
    all_to_all x1 -> x0, waiting for transfers between devices: 7.46 us -> none  [exchange(): lax.all_to_all(value.reshape(blocks, lanes, tokens), 'ctx', split_axis=0,...]
    dot_general x1 -> x0, matrix products: 7.25 us -> none  [body(): terms = jnp.dot(gated, out_weight, preferred_element_type=f32)]
    ppermute x1 -> x0, starting transfers between devices: 4.94 us -> none  [body(): lax.ppermute(qkv[:, tokens - 2:, :], 'ctx', [(i, i + 1) for i in range(bl...]
    unnamed x18 -> x1, local copies, waits for them, and re-layouts: 6.47 us -> 1.87 us
  transfers between devices with their start and end apart: 3 -> 0, of which waited for: 2 -> 0; matrix products, arithmetic and copies ran while one was open for 7% -> 0% of each run, Pallas kernels for 0% -> 0%
where the time goes in v2:
time: 79.8 us; the launch traced here: 79.6 us
  Pallas kernels  77.7 us (97%)
  local copies, waits for them, and re-layouts  1.87 us (2%)
    pallas_call x1, Pallas kernels, body(): pl.pallas_call(functools.partial(kernel, blocks, tps, lanes), out_shape=j...  77.7 us
    unnamed x1, local copies, waits for them, and re-layouts  1.87 us

profile of v2, /device:TPU:1, one launch (start us, length us, event | category | flops | bytes accessed | tf_op | source)
XLA Modules:
  0.0 79.6 jit_solution(2050593783793256854)
XLA Ops:
  0.0 77.7 %hyena.1 = bf16[256,1024]{1,0:T(8,128)(2,1)} custom-call(bf16[3,256,1024]{2,1,0:T(8,128)(2,1)} %qkv_hbm.1, f32[3,3,1024]{2,1,0:T(4,128)} %taps_ref.1, bf16[256,1024]{1,0:T(8,128)(2,1)} %filter_hbm.1, f32[1,1024]{1,0:T(1,128)} %bitcast.1, bf16[1024,4096]{1,0:T(8,128)(2,1)} %weight_hbm.1, bf16[2080,1024]{1,0:T(8,128)(2,1)} %constant.10.clone.lead_hbm, ...), custom_call_target="tpu_custom_call" | custom-call | tf_op jit(solution)/shard_map/hyena/pallas_call | solution.py:400
  77.8 1.9 %copy.12 = bf16[256,1024]{1,0:T(8,128)(2,1)} copy(bf16[256,1024]{1,0:T(8,128)(2,1)} %hyena.1) | data formatting | bytes 1048576

commit v3 on v2

--- a/solution.py
+++ b/solution.py
@@ -9,39 +9,29 @@
 from jax.sharding import PartitionSpec as P
 
 MESH = pl.DeviceIdType.MESH
-GROUP = 13
 LANE = 128
 HALO = 16
 
 
 def tables(blocks, width, lanes):
-    freqs = blocks + 1
+    f = np.arange(blocks)
     points = 2 * blocks * width
-    f = np.arange(freqs)
     angle = 2.0 * np.pi * np.outer(f, np.arange(blocks)) / (2 * blocks)
-    steps = freqs // GROUP
-    eye = np.eye(lanes)
-    pair = np.stack([np.cos(angle), -np.sin(angle)]).reshape(2, steps, GROUP, blocks)
-    pair = pair.transpose(1, 0, 2, 3).reshape(2 * freqs, blocks)
-    lead = np.kron(pair, eye)
-    weight = np.where((f == 0) | (f == blocks), 1.0, 2.0)[:, None] / points
-    turn = 2.0 * np.pi * np.outer(f, np.arange(width)) / points
-    twiddle = np.stack([np.cos(turn), -np.sin(turn)])
-    twiddle = np.repeat(twiddle, lanes, axis=1)
+    real, imag = np.cos(angle), -np.sin(angle)
+    imag[0] = np.cos(np.pi * f)
+    weight = np.where(f == 0, 1.0, 2.0)[:, None] / points
+    back_real, back_imag = real * weight, imag * weight
+    back_imag[0] = imag[0] / points
+    turn = 2.0 * np.pi * np.outer(np.minimum(np.arange(blocks + lanes), blocks), np.arange(width)) / points
     inner = 2.0 * np.pi * np.outer(np.arange(width), np.arange(width)) / width
     c, s = np.cos(inner), np.sin(inner)
-    forward = np.block([[c, -s], [s, c]])
-    backward = np.block([[c, s], [-s, c]])
-    scaled = np.stack([np.cos(angle) * weight, -np.sin(angle) * weight]).reshape(2, steps, GROUP, blocks)
-    scaled = scaled.transpose(1, 0, 2, 3).reshape(2 * freqs, blocks)
-    tail = np.kron(scaled.T, eye)
     half = jnp.bfloat16
     return (
-        lead.astype(half),
-        tail.astype(half),
-        twiddle.astype(np.float32),
-        forward.astype(half),
-        backward.astype(half),
+        np.concatenate([real, imag]).astype(half),
+        np.concatenate([back_real, back_imag]).T.astype(half),
+        np.stack([np.cos(turn), -np.sin(turn)]).astype(np.float32),
+        np.block([[c, -s], [s, c]]).astype(half),
+        np.block([[c, s], [-s, c]]).astype(half),
     )
 
 
@@ -80,7 +70,7 @@
     h_ref,
     x_ref,
     sh_ref,
-    back_ref,
+    wide_ref,
     y_ref,
     conv_ref,
     gated_ref,
@@ -219,92 +209,76 @@
     lax.fori_loop(0, chunks, query, 0)
 
     width = tokens
-    rows = GROUP * lanes
-    steps = (blocks + 1) // GROUP
-
-    def tables_at(i):
-        at = pl.ds(pl.multiple_of(i * rows, 16), rows)
-        at2 = pl.ds(pl.multiple_of(i * 2 * rows, 16), 2 * rows)
-        return at, at2, twiddle_ref[0, at, :], twiddle_ref[1, at, :]
-
-    def spectrum(ref, i):
-        _, at2, cos, sin = tables_at(i)
-        first = dot(lead_ref[at2, :], ref[...])
-        real, imag = first[:rows], first[rows:]
-        turned = jnp.concatenate([real * cos - imag * sin, real * sin + imag * cos], axis=1)
-        return dot(turned.astype(bf16), forward_ref[...])
+    first_row = lax.broadcasted_iota(jnp.int32, (blocks, width), 0) == 0
+    halves = (slice(0, half_tok), slice(half_tok, tokens))
+
+    def turns_of():
+        return twiddle_ref[0, :blocks], twiddle_ref[1, :blocks], twiddle_ref[0, blocks:], twiddle_ref[1, blocks:]
+
+    def spectrum(ref):
+        cos, sin, cos_last, sin_last = turns_of()
+        for h, part in enumerate(halves):
+            wide_ref[h] = ref[:, part].astype(f32)
+        turned, last = [], []
+        for c in range(lanes):
+            picked = pl.ds(c, blocks, stride=lanes)
+            column = jnp.concatenate([wide_ref[0, picked, :], wide_ref[1, picked, :]], axis=1).astype(bf16)
+            first = dot(lead_ref[...], column)
+            real, imag = first[:blocks], first[blocks:]
+            last.append(imag[0:1])
+            imag = jnp.where(first_row, 0.0, imag)
+            turned.append(jnp.concatenate([real * cos - imag * sin, real * sin + imag * cos], axis=1).astype(bf16))
+        last = jnp.concatenate(last, axis=0)
+        turned.append(jnp.concatenate([last * cos_last, last * sin_last], axis=1).astype(bf16))
+        return dot(jnp.concatenate(turned, axis=0), forward_ref[...])
 
     for load in loads[2:5]:
         load.wait()
     from_filter = settled(filter_t, h_ref, filter_sem)
     from_filter.wait_recv()
 
-    def filter_step(i, carry):
-        at = tables_at(i)[0]
-        sh_ref[at, :] = spectrum(h_ref, i).astype(bf16)
-        return carry
-
-    lax.fori_loop(0, steps, filter_step, 0)
+    sh_ref[...] = spectrum(h_ref).astype(bf16)
     for load in loads[5:]:
         load.wait()
     from_filter.wait_send()
     from_signal = settled(signal_t, x_ref, signal_sem)
     from_signal.wait_recv()
 
-    def signal_step(i, carry):
-        at, at2, cos, sin = tables_at(i)
-        sx = spectrum(x_ref, i)
-        xr, xi = sx[:, :width], sx[:, width:]
-        hr, hi = sh_ref[at, :width].astype(f32), sh_ref[at, width:].astype(f32)
-        product = jnp.concatenate([xr * hr - xi * hi, xr * hi + xi * hr], axis=1)
-        back = dot(product.astype(bf16), backward_ref[...])
-        br, bi = back[:, :width], back[:, width:]
-        out = jnp.concatenate([br * cos + bi * sin, bi * cos - br * sin], axis=0)
-        back_ref[at2, :] = out.astype(bf16)
-        return carry
-
-    lax.fori_loop(0, steps, signal_step, 0)
-
-    group = 16
-    big = group * lanes
-    turns = blocks // group
-
-    def send_conv(i, h):
-        first = lax.rem(me // group + i, turns) * group
-
-        def one(k, carry):
-            p = first + lax.rem(me + k, group)
-
-            @pl.when(p != me)
-            def _():
-                pltpu.make_async_remote_copy(
-                    piece(y_ref.at[h], p),
-                    piece(conv_ref.at[h], me),
-                    conv_send.at[h],
-                    conv_recv.at[h],
-                    device_id={"ctx": p},
-                    device_id_type=MESH,
-                ).start()
-
+    sx = spectrum(x_ref)
+    xr, xi = sx[:, :width], sx[:, width:]
+    hr, hi = sh_ref[:, :width].astype(f32), sh_ref[:, width:].astype(f32)
+    product = jnp.concatenate([xr * hr - xi * hi, xr * hi + xi * hr], axis=1).astype(bf16)
+    back = dot(product, backward_ref[...])
+    br, bi = back[:, :width], back[:, width:]
+    cos, sin, cos_last, sin_last = turns_of()
+    last = br[lanes * blocks :] * cos_last + bi[lanes * blocks :] * sin_last
+    for c in range(lanes):
+        at = slice(c * blocks, (c + 1) * blocks)
+        real, imag = br[at], bi[at]
+        imag_turned = jnp.where(first_row, last[c : c + 1], imag * cos - real * sin)
+        turned = jnp.concatenate([real * cos + imag * sin, imag_turned], axis=0).astype(bf16)
+        y = dot(tail_ref[...], turned)
+        for h, part in enumerate(halves):
+            wide_ref[h, pl.ds(c, blocks, stride=lanes), :] = y[:, part]
+
+    def send_conv(h):
+        def one(i, carry):
+            p = lax.rem(me + i, blocks)
+            pltpu.make_async_remote_copy(
+                piece(y_ref.at[h], p),
+                piece(conv_ref.at[h], me),
+                conv_send.at[h],
+                conv_recv.at[h],
+                device_id={"ctx": p},
+                device_id_type=MESH,
+            ).start()
             return carry
 
-        lax.fori_loop(0, group, one, 0)
-
-    def last_step(i, carry):
-        at = pl.ds(pl.multiple_of(lax.rem(me // group + i, turns) * big, 16), big)
-        y = dot(tail_ref[at, :], back_ref[...]).astype(bf16)
-        y_ref[0, at, :] = y[:, :half_tok]
-        y_ref[1, at, :] = y[:, half_tok:]
-        send_conv(i, 0)
-        return carry
-
-    lax.fori_loop(0, turns, last_step, 0)
-
-    def rest_step(i, carry):
-        send_conv(i, 1)
-        return carry
-
-    lax.fori_loop(0, turns, rest_step, 0)
+        lax.fori_loop(1, blocks, one, 0)
+
+    for h in range(2):
+        y_ref[h] = wide_ref[h].astype(bf16)
+        send_conv(h)
     from_conv = []
     for h in range(2):
         conv_ref[h, own, :] = y_ref[h, own, :]
@@ -326,7 +300,7 @@
             src, dst, tp_send.at[s], tp_recv.at[s], device_id={"tp": (right, left)[side]}, device_id_type=MESH
         )
 
-    def product(h, dest, start):
+    def project(h, dest, start):
         at = pl.ds(pl.multiple_of(dest * cols + start, half_col), half_col)
         return dot(gated_ref[h], weight_ref[:, at])
 
@@ -336,26 +310,23 @@
         from_conv[h].wait_recv()
         tok = pl.ds(h * half_tok, half_tok)
 
-        def gate(i, carry):
-            at = chunk_at(i)
+        for i in range(chunks):
+            at = slice(i * LANE, (i + 1) * LANE)
             conv = conv_ref[h, at, :].astype(f32).T
             signal = signal_ref[tok, at].astype(f32)
             gated_ref[h, :, at] = (query_ref[tok, at] * (conv + skip_ref[:, at] * signal)).astype(bf16)
-            return carry
-
-        lax.fori_loop(0, chunks, gate, 0)
         for side in range(2):
-            relay_src[h, side] = product(h, far, side * half_col).astype(bf16)
+            relay_src[h, side] = project(h, far, side * half_col).astype(bf16)
             copy = tp_copy(relay_src.at[h, side], relay_in.at[h, side], h, 0, side)
             copy.start()
             relays.append(copy)
         for side, dest in ((0, right), (1, left)):
-            send_ref[h, side, 1] = product(h, dest, (1 - side) * half_col).astype(bf16)
+            send_ref[h, side, 1] = project(h, dest, (1 - side) * half_col).astype(bf16)
             copy = tp_copy(send_ref.at[h, side, 1], take_ref.at[h, side, 1], h, 1, side)
             copy.start()
             opens.append(copy)
         for side, dest in ((0, right), (1, left)):
-            part_ref[side] = product(h, dest, side * half_col)
+            part_ref[side] = project(h, dest, side * half_col)
         for side in range(2):
             relays[2 * h + side].wait_recv()
             send_ref[h, side, 0] = (part_ref[side] + relay_in[h, side].astype(f32)).astype(bf16)
@@ -363,7 +334,7 @@
             copy.start()
             sums.append(copy)
         for part in range(2):
-            part_ref[2 + 2 * h + part] = product(h, col, part * half_col)
+            part_ref[2 + 2 * h + part] = project(h, col, part * half_col)
 
     for h in range(2):
         for side in range(2):
@@ -415,7 +386,7 @@
             pltpu.VMEM((channels, tokens), bf16),
             pltpu.VMEM((channels, tokens), bf16),
             pltpu.VMEM((freqs, 2 * tokens), bf16),
-            pltpu.VMEM((2 * freqs, tokens), bf16),
+            pltpu.VMEM((2, channels, half), f32),
             pltpu.VMEM((2, channels, half), bf16),
             pltpu.VMEM((2, channels, half), bf16),
             pltpu.VMEM((2, half, channels), bf16),

time: 79.8 us -> 75.1 us (0.941)
  Pallas kernels: 77.7 us -> 73.1 us
    pallas_call x1, Pallas kernels: 77.7 us -> 73.1 us  [body(): pl.pallas_call(functools.partial(kernel, blocks, tps, lanes), out_shape=j...]
where the time goes in v3:
time: 75.1 us; the launch traced here: 75 us
  Pallas kernels  73.1 us (97%)
  local copies, waits for them, and re-layouts  1.87 us (2%)
    pallas_call x1, Pallas kernels, body(): pl.pallas_call(functools.partial(kernel, blocks, tps, lanes), out_shape=j...  73.1 us
    unnamed x1, local copies, waits for them, and re-layouts  1.87 us

profile of v3, /device:TPU:1, one launch (start us, length us, event | category | flops | bytes accessed | tf_op | source)
XLA Modules:
  0.0 75.0 jit_solution(2147259913506425535)
XLA Ops:
  0.0 73.1 %hyena.1 = bf16[256,1024]{1,0:T(8,128)(2,1)} custom-call(bf16[3,256,1024]{2,1,0:T(8,128)(2,1)} %qkv_hbm.1, f32[3,3,1024]{2,1,0:T(4,128)} %taps_ref.1, bf16[256,1024]{1,0:T(8,128)(2,1)} %filter_hbm.1, f32[1,1024]{1,0:T(1,128)} %bitcast.1, bf16[1024,4096]{1,0:T(8,128)(2,1)} %weight_hbm.1, bf16[128,64]{1,0:T(8,128)(2,1)} %constant.10.clone.lead_hbm, ...), custom_call_target="tpu_custom_call" | custom-call | tf_op jit(solution)/shard_map/hyena/pallas_call | solution.py:371
  73.1 1.9 %copy.12 = bf16[256,1024]{1,0:T(8,128)(2,1)} copy(bf16[256,1024]{1,0:T(8,128)(2,1)} %hyena.1) | data formatting | bytes 1048576

commit v4 on v3

--- a/solution.py
+++ b/solution.py
@@ -10,6 +10,7 @@
 
 MESH = pl.DeviceIdType.MESH
 LANE = 128
+LINE = 16
 HALO = 16
 
 
@@ -65,6 +66,8 @@
     halo_ref,
     filter_t,
     signal_t,
+    filter_line,
+    signal_strip,
     signal_ref,
     query_ref,
     h_ref,
@@ -81,6 +84,9 @@
     take_ref,
     load_sem,
     halo_sem,
+    filter_send,
+    filter_recv,
+    signal_hop,
     filter_sem,
     signal_sem,
     conv_send,
@@ -105,17 +111,25 @@
 
     barrier = pltpu.get_barrier_semaphore()
 
+    ys = blocks // LINE
+    y = me // LINE
+    spot = lax.rem(me, LINE)
+    strip_rows = LINE * lanes
+
     def greet(i, carry):
-        pl.semaphore_signal(barrier, inc=1, device_id={"ctx": lax.rem(me + i, blocks)}, device_id_type=MESH)
+        peer = y * LINE + lax.rem(spot + i, LINE)
+        pl.semaphore_signal(barrier, inc=1, device_id={"ctx": peer}, device_id_type=MESH)
         return carry
 
-    lax.fori_loop(1, blocks, greet, 0)
+    lax.fori_loop(1, LINE, greet, 0)
+    for back_by in [LINE * dy for dy in range(1, ys)] + [1]:
+        peer = lax.rem(me + blocks - back_by, blocks)
+        pl.semaphore_signal(barrier, inc=1, device_id={"ctx": peer}, device_id_type=MESH)
     right = lax.rem(col + 1, tps)
     left = lax.rem(col + tps - 1, tps)
     for side in (left, right):
         pl.semaphore_signal(barrier, inc=1, device_id={"tp": side}, device_id_type=MESH)
 
-    per = LANE // lanes
     chunks = channels // LANE
 
     def piece(ref, p):
@@ -124,22 +138,40 @@
     def chunk_at(i):
         return pl.ds(pl.multiple_of(i * LANE, LANE), LANE)
 
-    def scatter(src, dst, sems, chunk):
-        def one(k, carry):
-            p = chunk * per + lax.rem(me + k, per)
-
-            @pl.when(p != me)
-            def _():
-                pltpu.make_async_remote_copy(
-                    piece(src, p), piece(dst, me), sems.at[0], sems.at[1], device_id={"ctx": p}, device_id_type=MESH
-                ).start()
-
+    def rows_of(block, count):
+        return pl.ds(pl.multiple_of(block * lanes, lanes), count * lanes)
+
+    def cross(src, strip, sems, dy):
+        to = lax.rem(y + dy, ys)
+        return pltpu.make_async_remote_copy(
+            src.at[rows_of(to * LINE, LINE)],
+            strip.at[dy - 1],
+            sems.at[0, dy - 1],
+            sems.at[1, dy - 1],
+            device_id={"ctx": to * LINE + spot},
+            device_id_type=MESH,
+        )
+
+    def along(src, first, dst, dst_sems, origin):
+        there = rows_of(origin * LINE + spot, 1)
+
+        def one(i, carry):
+            peer = lax.rem(spot + i, LINE)
+            pltpu.make_async_remote_copy(
+                src.at[rows_of(first + peer, 1)],
+                dst.at[there],
+                dst_sems.at[0],
+                dst_sems.at[1],
+                device_id={"ctx": y * LINE + peer},
+                device_id_type=MESH,
+            ).start()
             return carry
 
-        lax.fori_loop(0, per, one, 0)
-
-    def settled(src, dst, sems):
-        rows = (blocks - 1) * lanes
+        lax.fori_loop(1, LINE, one, 0)
+        dst[there, :] = src[rows_of(first + spot, 1), :]
+
+    def settled(src, dst, sems, pieces):
+        rows = pieces * lanes
         return pltpu.make_async_remote_copy(
             src.at[pl.ds(0, rows)],
             dst.at[pl.ds(0, rows)],
@@ -149,18 +181,18 @@
             device_id_type=MESH,
         )
 
-    own = pl.ds(pl.multiple_of(me * lanes, lanes), lanes)
+    own = rows_of(me, 1)
+    nearest = sorted(range(1, ys), key=lambda dy: min(dy, ys - dy))
 
     loads[0].wait()
 
-    def flip(i, carry):
-        at = chunk_at(i)
-        filter_t[at, :] = filter_ref[:, at].astype(f32).T.astype(bf16)
-        return carry
-
-    lax.fori_loop(0, chunks, flip, 0)
+    per = LANE // lanes
+    for i in range(chunks):
+        turned = filter_ref[:, i * LANE : (i + 1) * LANE].astype(f32).T.astype(bf16)
+        place = slice(i * per % LINE, i * per % LINE + per)
+        filter_t[i * per // LINE, place] = turned.reshape(per, lanes, tokens)
     loads[1].wait()
-    pl.semaphore_wait(barrier, blocks + 1)
+    pl.semaphore_wait(barrier, LINE + ys + 1)
 
     halo = pltpu.make_async_remote_copy(
         qkv_ref.at[:, pl.ds(tokens - HALO, HALO)],
@@ -172,12 +204,33 @@
     )
     halo.start()
 
-    def send_filter(i, carry):
-        scatter(filter_t, h_ref, filter_sem, lax.rem(me // per + i, chunks))
+    def along_filter(i, carry):
+        peer = lax.rem(spot + i, LINE)
+        pltpu.make_async_remote_copy(
+            filter_t.at[:, peer],
+            filter_line.at[i],
+            filter_send.at[0],
+            filter_recv.at[i],
+            device_id={"ctx": y * LINE + peer},
+            device_id_type=MESH,
+        ).start()
         return carry
 
-    lax.fori_loop(0, chunks, send_filter, 0)
-    h_ref[own, :] = filter_t[own, :]
+    def across_filter(src, origin):
+        for dy in range(1, ys):
+            to = lax.rem(y + dy, ys)
+            pltpu.make_async_remote_copy(
+                src.at[to],
+                h_ref.at[rows_of(y * LINE + origin, 1)],
+                filter_sem.at[0],
+                filter_sem.at[1],
+                device_id={"ctx": to * LINE + spot},
+                device_id_type=MESH,
+            ).start()
+
+    lax.fori_loop(1, LINE, along_filter, 0)
+    across_filter(filter_t.at[:, spot], spot)
+    h_ref[own, :] = filter_t[y, spot]
     halo.wait()
 
     def shortened(i, at):
@@ -189,17 +242,15 @@
             + taps_ref[i, 2:3, at] * wide[HALO - 2 : HALO - 2 + tokens]
         )
 
-    def send_signal(i, carry):
-        chunk = lax.rem(me // per + i, chunks)
-        at = chunk_at(chunk)
+    signal_cross = [cross(signal_t, signal_strip, signal_hop, dy) for dy in nearest]
+    for dy, copy in zip(nearest + [0], signal_cross + [None]):
+        at = rows_of(lax.rem(y + dy, ys) * LINE, LINE)
         signal = (shortened(1, at) * shortened(2, at)).astype(bf16)
         signal_ref[:, at] = signal
         signal_t[at, :] = signal.astype(f32).T.astype(bf16)
-        scatter(signal_t, x_ref, signal_sem, chunk)
-        return carry
-
-    lax.fori_loop(0, chunks, send_signal, 0)
-    x_ref[own, :] = signal_t[own, :]
+        if copy is not None:
+            copy.start()
+    along(signal_t, y * LINE, x_ref, signal_sem, y)
 
     def query(i, carry):
         at = chunk_at(i)
@@ -207,6 +258,31 @@
         return carry
 
     lax.fori_loop(0, chunks, query, 0)
+
+    def pass_signal(index):
+        dy = nearest[index]
+        signal_cross[index].wait_recv()
+        along(signal_strip.at[dy - 1], 0, x_ref, signal_sem, lax.rem(y + ys - dy, ys))
+
+    for index in range(ys - 2):
+        pass_signal(index)
+
+    def pass_filter(i, carry):
+        origin = lax.rem(spot + LINE - i, LINE)
+        pltpu.make_async_remote_copy(
+            filter_line.at[i],
+            filter_line.at[i],
+            filter_send.at[0],
+            filter_recv.at[i],
+            device_id={"ctx": me},
+            device_id_type=MESH,
+        ).wait_recv()
+        across_filter(filter_line.at[i], origin)
+        h_ref[rows_of(y * LINE + origin, 1), :] = filter_line[i, y]
+        return carry
+
+    lax.fori_loop(1, LINE, pass_filter, 0)
+    pass_signal(ys - 2)
 
     width = tokens
     first_row = lax.broadcasted_iota(jnp.int32, (blocks, width), 0) == 0
@@ -234,14 +310,23 @@
 
     for load in loads[2:5]:
         load.wait()
-    from_filter = settled(filter_t, h_ref, filter_sem)
+    from_filter = settled(x_ref, h_ref, filter_sem, (ys - 1) * LINE)
     from_filter.wait_recv()
 
     sh_ref[...] = spectrum(h_ref).astype(bf16)
     for load in loads[5:]:
         load.wait()
     from_filter.wait_send()
-    from_signal = settled(signal_t, x_ref, signal_sem)
+    sent = pl.ds(0, LINE - 1)
+    pltpu.make_async_remote_copy(
+        filter_line.at[sent],
+        filter_line.at[sent],
+        filter_send.at[0],
+        filter_recv.at[0],
+        device_id={"ctx": me},
+        device_id_type=MESH,
+    ).wait_send()
+    from_signal = settled(signal_t, x_ref, signal_sem, ys * (LINE - 1))
     from_signal.wait_recv()
 
     sx = spectrum(x_ref)
@@ -350,7 +435,7 @@
             out_ref[tok, pl.ds(part * half_col, half_col)] = total.astype(bf16)
 
     from_signal.wait_send()
-    for copy in from_conv + relays + opens + sums:
+    for copy in signal_cross + from_conv + relays + opens + sums:
         copy.wait_send()
 
 
@@ -359,6 +444,7 @@
     tps = lax.axis_size("tp")
     tokens, channels = qkv.shape[1:]
     lanes = channels // blocks
+    lines = blocks // LINE
     cols = out_weight.shape[1] // tps
     consts = [jnp.asarray(c) for c in tables(blocks, tokens, lanes)]
     freqs = (blocks + 1) * lanes
@@ -379,8 +465,10 @@
             pltpu.VMEM(out_weight.shape, bf16),
             *[pltpu.VMEM(c.shape, c.dtype) for c in consts],
             pltpu.VMEM((3, HALO, channels), bf16),
+            pltpu.VMEM((lines, LINE, lanes, tokens), bf16),
             pltpu.VMEM((channels, tokens), bf16),
-            pltpu.VMEM((channels, tokens), bf16),
+            pltpu.VMEM((LINE, lines, lanes, tokens), bf16),
+            pltpu.VMEM((lines - 1, LINE * lanes, tokens), bf16),
             pltpu.VMEM((tokens, channels), bf16),
             pltpu.VMEM((tokens, channels), f32),
             pltpu.VMEM((channels, tokens), bf16),
@@ -397,6 +485,9 @@
             pltpu.VMEM((2, 2, 2, half, cols // 2), bf16),
             dma((8,)),
             dma((2,)),
+            dma((1,)),
+            dma((LINE,)),
+            dma((2, lines - 1)),
             dma((2,)),
             dma((2,)),
             dma((2,)),

time: 75.1 us -> 72.1 us (0.960)
  Pallas kernels: 73.1 us -> 70.1 us
    pallas_call x1, Pallas kernels: 73.1 us -> 70.1 us  [body(): pl.pallas_call(functools.partial(kernel, blocks, tps, lanes), out_shape=j...]
where the time goes in v4:
time: 72.1 us; the launch traced here: 71.9 us
  Pallas kernels  70.1 us (97%)
  local copies, waits for them, and re-layouts  1.87 us (3%)
    pallas_call x1, Pallas kernels, body(): pl.pallas_call(functools.partial(kernel, blocks, tps, lanes), out_shape=j...  70.1 us
    unnamed x1, local copies, waits for them, and re-layouts  1.87 us

profile of v4, /device:TPU:1, one launch (start us, length us, event | category | flops | bytes accessed | tf_op | source)
XLA Modules:
  0.0 71.9 jit_solution(17433925026559909843)
XLA Ops:
  0.0 70.1 %hyena.1 = bf16[256,1024]{1,0:T(8,128)(2,1)} custom-call(bf16[3,256,1024]{2,1,0:T(8,128)(2,1)} %qkv_hbm.1, f32[3,3,1024]{2,1,0:T(4,128)} %taps_ref.1, bf16[256,1024]{1,0:T(8,128)(2,1)} %filter_hbm.1, f32[1,1024]{1,0:T(1,128)} %bitcast.1, bf16[1024,4096]{1,0:T(8,128)(2,1)} %weight_hbm.1, bf16[128,64]{1,0:T(8,128)(2,1)} %constant.10.clone.lead_hbm, ...), custom_call_target="tpu_custom_call" | custom-call | tf_op jit(solution)/shard_map/hyena/pallas_call | solution.py:457
  70.1 1.9 %copy.12 = bf16[256,1024]{1,0:T(8,128)(2,1)} copy(bf16[256,1024]{1,0:T(8,128)(2,1)} %hyena.1) | data formatting | bytes 1048576

commit v5 on v4

--- a/solution.py
+++ b/solution.py
@@ -152,23 +152,28 @@
             device_id_type=MESH,
         )
 
-    def along(src, first, dst, dst_sems, origin):
+    def along(src, first, dst, sems, origin, core):
         there = rows_of(origin * LINE + spot, 1)
 
         def one(i, carry):
-            peer = lax.rem(spot + i, LINE)
-            pltpu.make_async_remote_copy(
-                src.at[rows_of(first + peer, 1)],
-                dst.at[there],
-                dst_sems.at[0],
-                dst_sems.at[1],
-                device_id={"ctx": y * LINE + peer},
-                device_id_type=MESH,
-            ).start()
+            peer = 2 * lax.rem(spot // 2 + i, LINE // 2) + core
+
+            @pl.when(peer != spot)
+            def _():
+                pltpu.make_async_remote_copy(
+                    src.at[rows_of(first + peer, 1)],
+                    dst.at[there],
+                    sems.at[0],
+                    sems.at[1],
+                    device_id={"ctx": y * LINE + peer},
+                    device_id_type=MESH,
+                ).start()
+
             return carry
 
-        lax.fori_loop(1, LINE, one, 0)
-        dst[there, :] = src[rows_of(first + spot, 1), :]
+        lax.fori_loop(0, LINE // 2, one, 0)
+        if core == 0:
+            dst[there, :] = src[rows_of(first + spot, 1), :]
 
     def settled(src, dst, sems, pieces):
         rows = pieces * lanes
@@ -250,7 +255,7 @@
         signal_t[at, :] = signal.astype(f32).T.astype(bf16)
         if copy is not None:
             copy.start()
-    along(signal_t, y * LINE, x_ref, signal_sem, y)
+    along(signal_t, y * LINE, x_ref, signal_sem, y, 0)
 
     def query(i, carry):
         at = chunk_at(i)
@@ -259,13 +264,14 @@
 
     lax.fori_loop(0, chunks, query, 0)
 
-    def pass_signal(index):
+    def pass_signal(index, core):
         dy = nearest[index]
-        signal_cross[index].wait_recv()
-        along(signal_strip.at[dy - 1], 0, x_ref, signal_sem, lax.rem(y + ys - dy, ys))
+        if core == 0:
+            signal_cross[index].wait_recv()
+        along(signal_strip.at[dy - 1], 0, x_ref, signal_sem, lax.rem(y + ys - dy, ys), core)
 
     for index in range(ys - 2):
-        pass_signal(index)
+        pass_signal(index, 0)
 
     def pass_filter(i, carry):
         origin = lax.rem(spot + LINE - i, LINE)
@@ -282,7 +288,10 @@
         return carry
 
     lax.fori_loop(1, LINE, pass_filter, 0)
-    pass_signal(ys - 2)
+    pass_signal(ys - 2, 0)
+    along(signal_t, y * LINE, x_ref, signal_sem, y, 1)
+    for index in range(ys - 1):
+        pass_signal(index, 1)
 
     width = tokens
     first_row = lax.broadcasted_iota(jnp.int32, (blocks, width), 0) == 0
@@ -361,9 +370,9 @@
 
         lax.fori_loop(1, blocks, one, 0)
 
-    for h in range(2):
-        y_ref[h] = wide_ref[h].astype(bf16)
-        send_conv(h)
+    y_ref[0] = wide_ref[0].astype(bf16)
+    send_conv(0)
+    y_ref[1] = wide_ref[1].astype(bf16)
     from_conv = []
     for h in range(2):
         conv_ref[h, own, :] = y_ref[h, own, :]
@@ -390,52 +399,69 @@
         return dot(gated_ref[h], weight_ref[:, at])
 
     far = lax.rem(col + 2, tps)
-    relays, opens, sums = [], [], []
-    for h in range(2):
-        from_conv[h].wait_recv()
+    relays, opens, sums = {}, {}, {}
+
+    def gate(h):
         tok = pl.ds(h * half_tok, half_tok)
-
         for i in range(chunks):
             at = slice(i * LANE, (i + 1) * LANE)
             conv = conv_ref[h, at, :].astype(f32).T
             signal = signal_ref[tok, at].astype(f32)
             gated_ref[h, :, at] = (query_ref[tok, at] * (conv + skip_ref[:, at] * signal)).astype(bf16)
+
+    def relay(h):
         for side in range(2):
             relay_src[h, side] = project(h, far, side * half_col).astype(bf16)
-            copy = tp_copy(relay_src.at[h, side], relay_in.at[h, side], h, 0, side)
-            copy.start()
-            relays.append(copy)
+            relays[h, side] = tp_copy(relay_src.at[h, side], relay_in.at[h, side], h, 0, side)
+            relays[h, side].start()
+
+    def give(h):
         for side, dest in ((0, right), (1, left)):
             send_ref[h, side, 1] = project(h, dest, (1 - side) * half_col).astype(bf16)
-            copy = tp_copy(send_ref.at[h, side, 1], take_ref.at[h, side, 1], h, 1, side)
-            copy.start()
-            opens.append(copy)
+            opens[h, side] = tp_copy(send_ref.at[h, side, 1], take_ref.at[h, side, 1], h, 1, side)
+            opens[h, side].start()
+
+    def meet(h):
         for side, dest in ((0, right), (1, left)):
-            part_ref[side] = project(h, dest, side * half_col)
+            part_ref[h, side] = project(h, dest, side * half_col)
+
+    def add(h):
         for side in range(2):
-            relays[2 * h + side].wait_recv()
-            send_ref[h, side, 0] = (part_ref[side] + relay_in[h, side].astype(f32)).astype(bf16)
-            copy = tp_copy(send_ref.at[h, side, 0], take_ref.at[h, side, 0], h, 2, side)
-            copy.start()
-            sums.append(copy)
+            relays[h, side].wait_recv()
+            send_ref[h, side, 0] = (part_ref[h, side] + relay_in[h, side].astype(f32)).astype(bf16)
+            sums[h, side] = tp_copy(send_ref.at[h, side, 0], take_ref.at[h, side, 0], h, 2, side)
+            sums[h, side].start()
+
+    def keep(h):
         for part in range(2):
-            part_ref[2 + 2 * h + part] = project(h, col, part * half_col)
+            part_ref[h, 2 + part] = project(h, col, part * half_col)
+
+    for h in range(2):
+        from_conv[h].wait_recv()
+        if h == 0:
+            send_conv(1)
+        gate(h)
+        relay(h)
+        give(h)
+        meet(h)
+        add(h)
+        keep(h)
 
     for h in range(2):
         for side in range(2):
-            opens[2 * h + side].wait_recv()
-            sums[2 * h + side].wait_recv()
+            opens[h, side].wait_recv()
+            sums[h, side].wait_recv()
         tok = pl.ds(h * half_tok, half_tok)
         for part in range(2):
             total = (
-                part_ref[2 + 2 * h + part]
+                part_ref[h, 2 + part]
                 + take_ref[h, 0, part].astype(f32)
                 + take_ref[h, 1, 1 - part].astype(f32)
             )
             out_ref[tok, pl.ds(part * half_col, half_col)] = total.astype(bf16)
 
     from_signal.wait_send()
-    for copy in signal_cross + from_conv + relays + opens + sums:
+    for copy in [*signal_cross, *from_conv, *relays.values(), *opens.values(), *sums.values()]:
         copy.wait_send()
 
 
@@ -480,7 +506,7 @@
             pltpu.VMEM((2, half, channels), bf16),
             pltpu.VMEM((2, 2, half, cols // 2), bf16),
             pltpu.VMEM((2, 2, half, cols // 2), bf16),
-            pltpu.VMEM((6, half, cols // 2), f32),
+            pltpu.VMEM((2, 4, half, cols // 2), f32),
             pltpu.VMEM((2, 2, 2, half, cols // 2), bf16),
             pltpu.VMEM((2, 2, 2, half, cols // 2), bf16),
             dma((8,)),

time: 72.1 us -> 71.2 us (0.988)
  Pallas kernels: 70.1 us -> 69.2 us
    pallas_call x1, Pallas kernels: 70.1 us -> 69.2 us  [body(): pl.pallas_call(functools.partial(kernel, blocks, tps, lanes), out_shape=j...]
where the time goes in v5:
time: 71.2 us; the launch traced here: 71 us
  Pallas kernels  69.2 us (97%)
  local copies, waits for them, and re-layouts  1.87 us (3%)
    pallas_call x1, Pallas kernels, body(): pl.pallas_call(functools.partial(kernel, blocks, tps, lanes), out_shape=j...  69.2 us
    unnamed x1, local copies, waits for them, and re-layouts  1.87 us

profile of v5, /device:TPU:1, one launch (start us, length us, event | category | flops | bytes accessed | tf_op | source)
XLA Modules:
  0.0 71.0 jit_solution(12288403095577149890)
XLA Ops:
  0.0 69.2 %hyena.1 = bf16[256,1024]{1,0:T(8,128)(2,1)} custom-call(bf16[3,256,1024]{2,1,0:T(8,128)(2,1)} %qkv_hbm.1, f32[3,3,1024]{2,1,0:T(4,128)} %taps_ref.1, bf16[256,1024]{1,0:T(8,128)(2,1)} %filter_hbm.1, f32[1,1024]{1,0:T(1,128)} %bitcast.1, bf16[1024,4096]{1,0:T(8,128)(2,1)} %weight_hbm.1, bf16[128,64]{1,0:T(8,128)(2,1)} %constant.10.clone.lead_hbm, ...), custom_call_target="tpu_custom_call" | custom-call | tf_op jit(solution)/shard_map/hyena/pallas_call | solution.py:483
  69.2 1.9 %copy.12 = bf16[256,1024]{1,0:T(8,128)(2,1)} copy(bf16[256,1024]{1,0:T(8,128)(2,1)} %hyena.1) | data formatting | bytes 1048576

commit v6 on v5

--- a/solution.py
+++ b/solution.py
@@ -26,13 +26,15 @@
     turn = 2.0 * np.pi * np.outer(np.minimum(np.arange(blocks + lanes), blocks), np.arange(width)) / points
     inner = 2.0 * np.pi * np.outer(np.arange(width), np.arange(width)) / width
     c, s = np.cos(inner), np.sin(inner)
+    backward = np.block([[c, s], [-s, c]]).reshape(2 * width, 2, 2, width // 2).transpose(0, 2, 1, 3)
+    backward = backward.reshape(2 * width, 2 * width)
     half = jnp.bfloat16
     return (
         np.concatenate([real, imag]).astype(half),
         np.concatenate([back_real, back_imag]).T.astype(half),
         np.stack([np.cos(turn), -np.sin(turn)]).astype(np.float32),
         np.block([[c, -s], [s, c]]).astype(half),
-        np.block([[c, s], [-s, c]]).astype(half),
+        backward.astype(half),
     )
 
 
@@ -342,51 +344,58 @@
     xr, xi = sx[:, :width], sx[:, width:]
     hr, hi = sh_ref[:, :width].astype(f32), sh_ref[:, width:].astype(f32)
     product = jnp.concatenate([xr * hr - xi * hi, xr * hi + xi * hr], axis=1).astype(bf16)
-    back = dot(product, backward_ref[...])
-    br, bi = back[:, :width], back[:, width:]
     cos, sin, cos_last, sin_last = turns_of()
-    last = br[lanes * blocks :] * cos_last + bi[lanes * blocks :] * sin_last
-    for c in range(lanes):
-        at = slice(c * blocks, (c + 1) * blocks)
-        real, imag = br[at], bi[at]
-        imag_turned = jnp.where(first_row, last[c : c + 1], imag * cos - real * sin)
-        turned = jnp.concatenate([real * cos + imag * sin, imag_turned], axis=0).astype(bf16)
-        y = dot(tail_ref[...], turned)
-        for h, part in enumerate(halves):
-            wide_ref[h, pl.ds(c, blocks, stride=lanes), :] = y[:, part]
+
+    def invert(h):
+        part = halves[h]
+        back = dot(product, backward_ref[:, h * tokens : (h + 1) * tokens])
+        br, bi = back[:, :half_tok], back[:, half_tok:]
+        last = br[lanes * blocks :] * cos_last[:, part] + bi[lanes * blocks :] * sin_last[:, part]
+        for c in range(lanes):
+            at = slice(c * blocks, (c + 1) * blocks)
+            real, imag = br[at], bi[at]
+            imag_turned = jnp.where(first_row[:, part], last[c : c + 1], imag * cos[:, part] - real * sin[:, part])
+            turned = jnp.concatenate([real * cos[:, part] + imag * sin[:, part], imag_turned], axis=0).astype(bf16)
+            wide_ref[h, pl.ds(c, blocks, stride=lanes), :] = dot(tail_ref[...], turned)
+        y_ref[h] = wide_ref[h].astype(bf16)
+
+    waves = ((1, LINE + 1), (LINE + 1, blocks))
 
     def send_conv(h):
-        def one(i, carry):
-            p = lax.rem(me + i, blocks)
-            pltpu.make_async_remote_copy(
-                piece(y_ref.at[h], p),
-                piece(conv_ref.at[h], me),
-                conv_send.at[h],
-                conv_recv.at[h],
-                device_id={"ctx": p},
-                device_id_type=MESH,
-            ).start()
-            return carry
-
-        lax.fori_loop(1, blocks, one, 0)
-
-    y_ref[0] = wide_ref[0].astype(bf16)
+        for wave, (start, stop) in enumerate(waves):
+
+            def one(i, carry, slot=2 * h + wave):
+                p = lax.rem(me + i, blocks)
+                pltpu.make_async_remote_copy(
+                    piece(y_ref.at[h], p),
+                    piece(conv_ref.at[h], me),
+                    conv_send.at[slot],
+                    conv_recv.at[slot],
+                    device_id={"ctx": p},
+                    device_id_type=MESH,
+                ).start()
+                return carry
+
+            lax.fori_loop(start, stop, one, 0)
+
+    invert(0)
     send_conv(0)
-    y_ref[1] = wide_ref[1].astype(bf16)
+    invert(1)
     from_conv = []
     for h in range(2):
         conv_ref[h, own, :] = y_ref[h, own, :]
-        rows_all = pl.ds(0, (blocks - 1) * lanes)
-        from_conv.append(
-            pltpu.make_async_remote_copy(
-                y_ref.at[h, rows_all],
-                conv_ref.at[h, rows_all],
-                conv_send.at[h],
-                conv_recv.at[h],
-                device_id={"ctx": me},
-                device_id_type=MESH,
+        for wave, (start, stop) in enumerate(waves):
+            some = pl.ds(0, (stop - start) * lanes)
+            from_conv.append(
+                pltpu.make_async_remote_copy(
+                    y_ref.at[h, some],
+                    conv_ref.at[h, some],
+                    conv_send.at[2 * h + wave],
+                    conv_recv.at[2 * h + wave],
+                    device_id={"ctx": me},
+                    device_id_type=MESH,
+                )
             )
-        )
 
     def tp_copy(src, dst, h, kind, side):
         s = (h * 3 + kind) * 2 + side
@@ -437,9 +446,10 @@
             part_ref[h, 2 + part] = project(h, col, part * half_col)
 
     for h in range(2):
-        from_conv[h].wait_recv()
+        from_conv[2 * h].wait_recv()
         if h == 0:
             send_conv(1)
+        from_conv[2 * h + 1].wait_recv()
         gate(h)
         relay(h)
         give(h)
@@ -516,8 +526,8 @@
             dma((2, lines - 1)),
             dma((2,)),
             dma((2,)),
-            dma((2,)),
-            dma((2,)),
+            dma((4,)),
+            dma((4,)),
             dma((12,)),
             dma((12,)),
         ],

time: 71.2 us -> 70.2 us (0.986)
  Pallas kernels: 69.2 us -> 68.2 us
    pallas_call x1, Pallas kernels: 69.2 us -> 68.2 us  [body(): pl.pallas_call(functools.partial(kernel, blocks, tps, lanes), out_shape=j...]
where the time goes in v6:
time: 70.2 us; the launch traced here: 70 us
  Pallas kernels  68.2 us (97%)
  local copies, waits for them, and re-layouts  1.87 us (3%)
    pallas_call x1, Pallas kernels, body(): pl.pallas_call(functools.partial(kernel, blocks, tps, lanes), out_shape=j...  68.2 us
    unnamed x1, local copies, waits for them, and re-layouts  1.87 us

profile of v6, /device:TPU:1, one launch (start us, length us, event | category | flops | bytes accessed | tf_op | source)
XLA Modules:
  0.0 70.0 jit_solution(5894767394727475565)
XLA Ops:
  0.0 68.2 %hyena.1 = bf16[256,1024]{1,0:T(8,128)(2,1)} custom-call(bf16[3,256,1024]{2,1,0:T(8,128)(2,1)} %qkv_hbm.1, f32[3,3,1024]{2,1,0:T(4,128)} %taps_ref.1, bf16[256,1024]{1,0:T(8,128)(2,1)} %filter_hbm.1, f32[1,1024]{1,0:T(1,128)} %bitcast.1, bf16[1024,4096]{1,0:T(8,128)(2,1)} %weight_hbm.1, bf16[128,64]{1,0:T(8,128)(2,1)} %constant.10.clone.lead_hbm, ...), custom_call_target="tpu_custom_call" | custom-call | tf_op jit(solution)/shard_map/hyena/pallas_call | solution.py:493
  68.2 1.9 %copy.12 = bf16[256,1024]{1,0:T(8,128)(2,1)} copy(bf16[256,1024]{1,0:T(8,128)(2,1)} %hyena.1) | data formatting | bytes 1048576

commit v7 on v6

--- a/solution.py
+++ b/solution.py
@@ -492,7 +492,7 @@
     half = tokens // 2
     return pl.pallas_call(
         functools.partial(kernel, blocks, tps, lanes),
-        out_shape=jax.ShapeDtypeStruct((tokens, cols), bf16),
+        out_shape=pltpu.VMEM((tokens, cols), bf16),
         in_specs=[hbm, vmem, hbm, vmem] + [hbm] * 6,
         out_specs=vmem,
         scratch_shapes=[

time: 70.2 us -> 68.3 us (0.973)
  local copies, waits for them, and re-layouts: 1.87 us -> 0.8 us
  Pallas kernels: 68.2 us -> 67.4 us
    unnamed x1, local copies, waits for them, and re-layouts: 1.87 us -> 0.8 us
    pallas_call x1, Pallas kernels: 68.2 us -> 67.4 us  [body(): pl.pallas_call(functools.partial(kernel, blocks, tps, lanes), out_shape=p...]
where the time goes in v7:
time: 68.3 us; the launch traced here: 68.2 us
  Pallas kernels  67.4 us (99%)
  local copies, waits for them, and re-layouts  0.8 us (1%)
    pallas_call x1, Pallas kernels, body(): pl.pallas_call(functools.partial(kernel, blocks, tps, lanes), out_shape=p...  67.4 us

profile of v7, /device:TPU:1, one launch (start us, length us, event | category | flops | bytes accessed | tf_op | source)
XLA Modules:
  0.0 68.2 jit_solution(1007384328243211747)
XLA Ops:
  0.0 67.4 %hyena.1 = bf16[256,1024]{1,0:T(8,128)(2,1)S(1)} custom-call(bf16[3,256,1024]{2,1,0:T(8,128)(2,1)} %qkv_hbm.1, f32[3,3,1024]{2,1,0:T(4,128)} %taps_ref.1, bf16[256,1024]{1,0:T(8,128)(2,1)} %filter_hbm.1, f32[1,1024]{1,0:T(1,128)} %bitcast.1, bf16[1024,4096]{1,0:T(8,128)(2,1)} %weight_hbm.1, bf16[128,64]{1,0:T(8,128)(2,1)} %constant.10.clone.lead_hbm, ...), custom_call_target="tpu_custom_call" | custom-call | tf_op jit(solution)/shard_map/hyena/pallas_call | solution.py:493
  67.4 0.8 %copy.12 = bf16[256,1024]{1,0:T(8,128)(2,1)} copy(bf16[256,1024]{1,0:T(8,128)(2,1)S(1)} %hyena.1) | data formatting | bytes 1048576
